TPU v7x, 32 devices: a whole 2x2x4 slice. The times are simulated.
32 devices in a mesh: groups: 2 (over y), tok: 4 (over z), head: 4 (over x, core).
Axes of the slice: x: 2, y: 2, z: 4, core: 2. Of those that a mesh axis runs over, the one named last changes fastest.
Arguments:
- queries: bfloat16 [2048, 2048], P(('groups', 'tok'), 'head'), parts along dimension 0, may hold values from -8 to 8
- keys: bfloat16 [2048, 2048], P(('groups', 'tok'), 'head'), parts along dimension 0, may hold values from -8 to 8
- values: bfloat16 [2048, 2048], P(('groups', 'tok'), 'head'), parts along dimension 0, may hold values from -8 to 8
- fast_in: bfloat16 [4, 512, 1024], P('head'), may hold values from -0.25 to 0.25
- fast_out: bfloat16 [4, 512, 512], P('head'), may hold values from -0.25 to 0.25
- key_gain: float32 [4], P('head'), may hold values from 0.35 to 1.4
- out_proj: bfloat16 [2048, 4096], P('head', 'tok'), may hold values from -2 to 2
- grad_out: bfloat16 [2048, 4096], P(('groups', 'tok')), parts along dimension 0, may hold values from -12 to 12
Outputs:
- d_queries: bfloat16 [2048, 2048], P(('groups', 'tok'), 'head'), parts along dimension 0
- d_keys: bfloat16 [2048, 2048], P(('groups', 'tok'), 'head'), parts along dimension 0
- d_values: bfloat16 [2048, 2048], P(('groups', 'tok'), 'head'), parts along dimension 0
There are 2 independent parts, one for each index of `groups`. A program takes and returns all parts, laid end to end along the dimension named above; an argument that names none is the same for every part. Nothing has to cross between parts.
All inputs are finite; a program needn't handle non-finite values.
Results may differ from a plain program's by a relative error of at most 0.0012.
Values may be sent and summed in bfloat16 or wider, within the bound.
No kernel may reach another device: no remote copies, remote signals or barrier semaphores. Data moves between devices by JAX's collectives and lax.ppermute only.
A program may use at most 64 MiB of HBM per device.

v0:
```python
from functools import partial

import jax
import jax.numpy as jnp
from jax import lax
from jax.sharding import PartitionSpec as P

highest = lax.Precision.HIGHEST
inner_rate = 0.02
norm_eps = 1e-06


def fast_apply(weights, inputs):
    w_both, w_down = weights
    half_width = w_down.shape[0]
    mixed = jnp.dot(inputs, w_both, precision=highest)
    hidden = jax.nn.silu(mixed[:, :half_width]) * mixed[:, half_width:]
    return jnp.dot(hidden, w_down, precision=highest)


def inner_loss(weights, inputs, targets):
    misfit = fast_apply(weights, inputs) - targets
    return 0.5 * jnp.sum(misfit * misfit)


def inner_grad(weights, inputs, targets):
    return jax.grad(inner_loss)(weights, inputs, targets)


def query_pull(weights, inputs, cotangent):
    _, pullback = jax.vjp(fast_apply, weights, inputs)
    return pullback(cotangent)


def key_pull(weights, inputs, targets, cotangent):
    _, pullback = jax.vjp(partial(inner_grad, weights), inputs, targets)
    return pullback(cotangent)


def split_heads(array, heads):
    return array.reshape(array.shape[0], heads, -1).transpose(1, 0, 2).astype(jnp.float32)


def join_heads(array):
    return array.transpose(1, 0, 2).reshape(array.shape[1], -1).astype(jnp.bfloat16)


def frobenius(former, latter):
    return jnp.sum(former[0] * latter[0]) + jnp.sum(former[1] * latter[1])


def per_device(queries, keys, values, fast_in, fast_out, key_gain, out_proj, grad_out):
    heads_here = key_gain.shape[0]
    gain_col = key_gain[:, None, None]
    query_heads = split_heads(queries, heads_here)
    key_heads = split_heads(keys, heads_here) * gain_col
    value_heads = split_heads(values, heads_here)
    weights = (fast_in.astype(jnp.float32), fast_out.astype(jnp.float32))
    entries = (
        lax.axis_size("head")
        * heads_here
        * (fast_in.shape[1] * fast_in.shape[2] + fast_out.shape[1] * fast_out.shape[2])
    )
    out_grad = lax.dot_general(
        grad_out,
        lax.all_gather(out_proj, "tok", axis=1, tiled=True),
        (((1,), (1,)), ((), ())),
        preferred_element_type=jnp.float32,
    )
    out_heads = split_heads(out_grad, heads_here)
    partial_grad = jax.vmap(inner_grad)(weights, key_heads, value_heads)
    full_grad = lax.psum(partial_grad, "tok")
    square_sum = lax.psum(frobenius(full_grad, full_grad), "head")
    grad_rms = jnp.sqrt(square_sum / entries)
    denom = grad_rms + norm_eps
    updated = tuple(
        (member_w - inner_rate * member_g / denom for member_w, member_g in zip(weights, full_grad))
    )
    adjoint_local, query_grad = jax.vmap(query_pull)(updated, query_heads, out_heads)
    adjoint = lax.psum(adjoint_local, "tok")
    product = lax.psum(frobenius(full_grad, adjoint), "head")
    grad_adjoint = tuple(
        (
            -inner_rate
            * (member_a / denom - member_g * product / (denom * denom * entries * grad_rms))
            for member_a, member_g in zip(adjoint, full_grad)
        )
    )
    key_grad, value_grad = jax.vmap(key_pull)(weights, key_heads, value_heads, grad_adjoint)
    return (join_heads(query_grad), join_heads(key_grad * gain_col), join_heads(value_grad))


def solution(mesh):
    return jax.shard_map(
        per_device,
        mesh=mesh,
        in_specs=(
            P(("groups", "tok"), "head"),
            P(("groups", "tok"), "head"),
            P(("groups", "tok"), "head"),
            P("head", None, None),
            P("head", None, None),
            P("head"),
            P("head", "tok"),
            P(("groups", "tok"), None),
        ),
        out_specs=(
            P(("groups", "tok"), "head"),
            P(("groups", "tok"), "head"),
            P(("groups", "tok"), "head"),
        ),
        check_vma=False,
    )
```

profile of v0, /device:TPU:0, one launch (start us, length us, event | category | flops | bytes accessed | tf_op | source)
XLA Modules:
  0.0 399.2 jit_solution(3210539769428566195)
XLA Ops:
  7.2 0.0 copy-start
  7.2 0.0 copy-start.6
  7.2 0.0 copy-start.19
  7.2 0.0 all-reduce.13.cloned.1.call-start
  8.0 2.3 convolution_bitcast_fusion.4
  10.4 0.0 copy-done.6
  10.4 0.0 copy-done.19
  10.4 0.0 copy-start.12
  10.4 0.7 fusion.18
  11.1 0.0 copy-start.21
  11.1 2.1 convolution_bitcast_fusion.3
  13.2 0.0 copy-done.12
  13.2 1.5 fusion.89
  14.8 0.0 copy-done.21
  14.8 0.8 copy-done.10
  15.6 0.0 copy-done.5
  15.6 3.2 convolution_bitcast_fusion
  18.8 0.0 all-reduce.13.cloned.1.call-update
  18.8 0.0 copy-done.8
  18.9 0.0 all-gather.2.cloned.1.call-start
  18.9 0.7 all-gather.2.cloned.1.call-update
  19.6 0.0 copy-start.2
  19.6 0.0 all-reduce.11.cloned.1.call-start
  19.7 2.1 copy.13
  21.8 121.3 %all-reduce.13.cloned.1.call-done = (f32[1,512,512]{1,2,0:T(8,128)}, f32[1,512,1024]{1,2,0:T(8,128)}) async-done(((f32[1,512,512]{1,2,0:T(8,128)}, f32[1,512,1024]{1,2,0:T(8,128)}), (f32[1,512,512]{1,2,0:T(8,128)}, f32[1,512,1024]{1,2,0:T(8,128)})) %all-reduce.13.cloned.1.call-update) | async-done | bytes 3145744 | tf_op jit(solution)/shard_map/psum | solution.py:72
  143.1 2.1 multiply_reduce_fusion.3
  145.2 2.7 multiply_reduce_fusion.1
  149.2 0.0 copy-done.2
  149.2 1.4 copy.11
  150.6 7.5 %psum.44 = f32[]{:T(128)} all-reduce(f32[]{:T(128)S(6)} %add.46), channel_id=1, replica_groups=mesh['groups'=2,'tok'=4,'head'=4] {'head'}, use_global_device_ids=true, to_apply=%region_4.5 | all-reduce | flops 1 | bytes 8 | tf_op jit(solution)/shard_map/psum | solution.py:73
  158.8 4.4 %fusion.8 = f32[1,256,1024]{2,1,0:T(8,128)} fusion(bf16[256,512]{1,0:T(8,128)(2,1)} %param.8, f32[1,512,1024]{1,2,0:T(8,128)} %get-tuple-element.9, bf16[1,512,1024]{1,2,0:T(8,128)(2,1)} %copy.11, f32[]{:T(128)S(6)} %add.47), kind=kOutput, calls=%fused_computation.14 | convolution fusion | flops 1612709888 | bytes 4456452 | tf_op jit(solution)/shard_map/vmap(jvp())/dot_general | solution.py:16
  163.3 61.2 %all-gather.2.cloned.1.call-done = bf16[512,4096]{1,0:T(8,128)(2,1)} async-done(((bf16[512,1024]{1,0:T(8,128)(2,1)}), bf16[512,4096]{1,0:T(8,128)(2,1)}) %all-gather.2.cloned.1.call-update) | async-done | bytes 4194320 | tf_op jit(solution)/shard_map/all_gather | solution.py:66
  224.5 0.0 copy-done
  224.5 3.6 fusion.90
  228.0 0.0 copy-done.20
  228.1 0.0 copy-start.3
  228.1 0.0 copy-start.15
  228.1 2.2 convolution_bitcast_fusion.2
  230.2 1.3 fusion.79
  231.6 0.8 copy-done.16
  232.4 0.2 copy-done.17
  232.6 2.4 convolution_bitcast_fusion.1
  234.9 0.0 all-reduce.11.cloned.1.call-update
  234.9 120.1 %all-reduce.11.cloned.1.call-done = (f32[1,512,1024]{1,2,0:T(8,128)}, f32[1,512,512]{1,2,0:T(8,128)}) async-done(((f32[1,512,1024]{1,2,0:T(8,128)}, f32[1,512,512]{1,2,0:T(8,128)}), (f32[1,512,1024]{1,2,0:T(8,128)}, f32[1,512,512]{1,2,0:T(8,128)})) %all-reduce.11.cloned.1.call-update) | async-done | bytes 3145744 | tf_op jit(solution)/shard_map/psum | solution.py:80
  355.0 2.6 multiply_reduce_fusion.2
  357.6 2.7 multiply_reduce_fusion
  361.6 5.0 %fusion.26 = bf16[256,512]{1,0:T(8,128)(2,1)} fusion(f32[1,256,512]{2,1,0:T(8,128)} %copy-done.17, f32[1,256,512]{2,1,0:T(8,128)} %copy-done.16, f32[1,512,1024]{1,2,0:T(8,128)} %get-tuple-element.9, bf16[1,512,1024]{1,2,0:T(8,128)(2,1)} %copy.11, f32[]{:T(128)S(6)} %add.47), kind=kOutput, calls=%fused_computation.37 | convolution fusion | flops 1613103104 | bytes 4456452 | tf_op jit(solution)/shard_map/vmap(transpose(jvp()))/dot_general | solution.py:16
  366.7 7.6 %psum.47 = f32[]{:T(128)} all-reduce(f32[]{:T(128)S(6)} %add.49), channel_id=1, replica_groups=mesh['groups'=2,'tok'=4,'head'=4] {'head'}, use_global_device_ids=true, to_apply=%region_9.10 | all-reduce | flops 1 | bytes 8 | tf_op jit(solution)/shard_map/psum | solution.py:81
  374.3 3.4 subtract_multiply_fusion
  377.7 3.5 fusion.14
  381.2 0.0 copy-start.7
  381.2 0.0 copy-start.13
  381.3 2.1 fusion.11
  383.4 0.8 convolution_bitcast_fusion.10
  384.2 0.4 copy-done.4
  384.6 0.3 copy-done.14
  384.9 2.0 fusion.24
  386.9 0.0 copy-start.22
  386.9 0.0 copy-start.23
  386.9 0.7 fusion.74
  387.6 0.6 convolution_bitcast_fusion.9
  388.3 2.4 multiply_add_fusion
  390.7 1.1 fusion.29
  391.8 0.8 copy.18
  (22 shorter events, 0.0 us)
Async XLA Ops:
  7.2 217.3 %copy-start = (bf16[256,4096]{1,0:T(8,128)(2,1)S(1)}, bf16[256,4096]{1,0:T(8,128)(2,1)}, u32[]{:S(2)}) copy-start(bf16[256,4096]{1,0:T(8,128)(2,1)} %param.15) | copy-start | bytes 6291460
  7.2 3.2 copy-start.6
  7.2 3.2 copy-start.19
  7.2 135.9 %all-reduce.13.cloned.1.call-start = ((), (), s32[]{:S(2)}) async-start(), calls=%async_computation.2 | async-start | bytes 6291456 | tf_op jit(solution)/shard_map/psum | solution.py:72
  10.4 2.8 copy-start.12
  11.1 3.7 copy-start.21
  13.2 2.4 copy-start.5
  14.8 0.8 copy-start.10
  14.8 4.1 %copy-start.8 = (f32[1,256,512]{2,1,0:T(8,128)}, f32[1,256,512]{2,1,0:T(8,128)S(1)}, u32[]{:S(2)}) copy-start(f32[1,256,512]{2,1,0:T(8,128)S(1)} %get-tuple-element.14) | copy-start | bytes 1572868
  18.9 205.6 %all-gather.2.cloned.1.call-start = ((), (), s32[]{:S(2)}) async-start(), calls=%async_computation | async-start | bytes 5242880 | tf_op jit(solution)/shard_map/all_gather | solution.py:66
  19.6 129.6 %copy-start.2 = (bf16[1,512,1024]{2,1,0:T(8,128)(2,1)S(1)}, bf16[1,512,1024]{2,1,0:T(8,128)(2,1)}, u32[]{:S(2)}) copy-start(bf16[1,512,1024]{2,1,0:T(8,128)(2,1)} %param.11) | copy-start | bytes 3145732
  19.6 335.4 %all-reduce.11.cloned.1.call-start = ((), (), s32[]{:S(2)}) async-start(), calls=%async_computation.1 | async-start | bytes 6291456 | tf_op jit(solution)/shard_map/psum | solution.py:80
  224.5 3.6 copy-start.20
  228.1 2.2 copy-start.3
  228.1 2.2 copy-start.15
  230.2 2.3 copy-start.18
  231.6 0.8 copy-start.16
  231.6 1.0 copy-start.17
  355.0 2.6 copy-start.1
  374.3 3.5 copy-start.9
  374.3 3.5 copy-start.11
  381.2 2.1 copy-start.7
  381.2 2.1 copy-start.13
  383.4 1.2 copy-start.4
  383.4 1.5 copy-start.14
  386.9 1.4 copy-start.22
  386.9 1.4 copy-start.23
Sparse Core Ops, SparseCore 0:
  19.0 124.0 all-reduce.12
  144.7 79.7 all-gather.1
  235.1 119.9 all-reduce.10
where the time goes:
time: 400 us; the launch traced here: 399 us
  waiting for transfers between devices  303 us (76%)
  matrix products  41.2 us (10%)
  between operations  18.2 us (5%)
  blocking collectives  15.1 us (4%)
  other arithmetic  14.3 us (4%)
  local copies, waits for them, and re-layouts  6.95 us (2%)
    psum x1, waiting for transfers between devices, per_device(): full_grad = lax.psum(partial_grad, 'tok')  121 us
    psum x1, waiting for transfers between devices, per_device(): adjoint = lax.psum(adjoint_local, 'tok')  120 us
    all_gather x1, waiting for transfers between devices, per_device(): lax.all_gather(out_proj, 'tok', axis=1, tiled=True)  61.2 us
    dot_general x8, matrix products, fast_apply(): mixed = jnp.dot(inputs, w_both, precision=highest)  24 us
    dot_general x9, matrix products, fast_apply(): return jnp.dot(hidden, w_down, precision=highest)  13.7 us
    reduce_sum x4, other arithmetic, frobenius(): return jnp.sum(former[0] * latter[0]) + jnp.sum(former[1] * latter[1])  10.1 us
  transfers between devices with their start and end apart: 3, of which 3 were waited for; matrix products, arithmetic and copies ran while one was open for 3% of the time, Pallas kernels for 0%

commit v1 on v0

v1 whole, which is shorter than its diff:
```python
from functools import partial

import jax
import jax.numpy as jnp
from jax import lax
from jax.experimental import pallas as pl
from jax.experimental.pallas import tpu as pltpu
from jax.sharding import PartitionSpec as P

f32 = jnp.float32
bf16 = jnp.bfloat16
inner_rate = 0.02
norm_eps = 1e-06
vmem_bytes = 56 * 1024 * 1024
MIB = 1024 * 1024


def halves(x):
    top = x.astype(bf16)
    return top, (x - top.astype(f32)).astype(bf16)


def nn(a, b):
    return lax.dot_general(a, b, (((1,), (0,)), ((), ())), preferred_element_type=f32)


def nt(a, b):
    return lax.dot_general(a, b, (((1,), (1,)), ((), ())), preferred_element_type=f32)


def tn(a, b):
    return lax.dot_general(a, b, (((0,), (0,)), ((), ())), preferred_element_type=f32)


def two(dot, a, b):
    return dot(a[0], b) + dot(a[1], b)


def two_right(dot, a, b):
    return dot(a, b[0]) + dot(a, b[1])


def three(dot, a, b):
    return dot(a[0], b[0]) + dot(a[0], b[1]) + dot(a[1], b[0])


def sigmoid(u):
    return 1.0 / (1.0 + jnp.exp(-u))


def fetch_all(slots, held, sems):
    for j, slot in enumerate(slots):
        pltpu.make_async_copy(slot, held.at[j], sems.at[j]).start()


def inner_grad_kernel(count, keep, *refs):
    slots = refs[:count]
    gain_ref, wa_ref, wb_ref, ga_ref, gb_ref, sq_ref = refs[count : count + 6]
    held, sems = refs[-2:]
    fetch_all(slots, held, sems)
    gain = gain_ref[0]
    width = wb_ref.shape[0]
    ga_ref[...] = jnp.zeros_like(ga_ref)
    gb_ref[...] = jnp.zeros_like(gb_ref)

    @pl.loop(0, count)
    def _(j):
        pltpu.make_async_copy(slots[0], held.at[j], sems.at[j]).wait()
        keys = held[j, :, :width]
        values = held[j, :, width : 2 * width].astype(f32)
        mixed = nn(keys, wa_ref[...]) * gain
        u, w = mixed[:, :width], mixed[:, width:]
        sg = sigmoid(u)
        act = u * sg
        hidden = halves(act * w)
        e = two(nn, hidden, wb_ref[...]) - values
        e2 = halves(e)
        hb = two(nt, e2, wb_ref[...])
        if keep:
            e_ref, hb_ref = refs[count + 6 : count + 8]
            e_ref[j] = e
            hb_ref[j] = hb
        gb_ref[...] += three(tn, hidden, e2)
        slope = sg * (1.0 + u * (1.0 - sg))
        ga_ref[:, :width] += two_right(tn, keys, halves(hb * w * slope))
        ga_ref[:, width:] += two_right(tn, keys, halves(hb * act))

    ga = ga_ref[...] * gain
    ga_ref[...] = ga
    gb = gb_ref[...]
    sq_ref[...] = jnp.zeros_like(sq_ref) + (jnp.sum(ga * ga) + jnp.sum(gb * gb))


def vmem_spec():
    return pl.BlockSpec(memory_space=pltpu.VMEM)


def any_spec():
    return pl.BlockSpec(memory_space=pl.ANY)


def smem_spec():
    return pl.BlockSpec(memory_space=pltpu.SMEM)


def shape_of(*dims, dtype=f32):
    return jax.ShapeDtypeStruct(dims, dtype)


def estimate(units, rows):
    return pl.CostEstimate(
        flops=units * 2 * rows * 512 * 512, bytes_accessed=8 * MIB, transcendentals=0
    )


def call_inner_grad(slots, keep, gain, wa, wb):
    count = len(slots)
    kept = 2 if keep else 0
    rows, width = slots[0].shape[0], wb.shape[0]
    return pl.pallas_call(
        partial(inner_grad_kernel, count, keep),
        out_shape=(shape_of(width, 2 * width), shape_of(width, width), shape_of(8, 128))
        + (shape_of(count, rows, width),) * kept,
        in_specs=[any_spec()] * count + [smem_spec(), vmem_spec(), vmem_spec()],
        out_specs=[vmem_spec()] * (3 + kept),
        scratch_shapes=[
            pltpu.VMEM((count,) + slots[0].shape, bf16),
            pltpu.SemaphoreType.DMA((count,)),
        ],
        compiler_params=pltpu.CompilerParams(vmem_limit_bytes=vmem_bytes),
        cost_estimate=estimate(13, rows * count),
        name="inner_grad",
    )(*slots, gain, wa, wb)


def scale_of(sums, entries):
    total = sums[0][0:1, 0:1]
    for more in sums[1:]:
        total = total + more[0:1, 0:1]
    rms = jnp.sqrt(total / entries)
    return rms, rms + norm_eps


def query_kernel(count, n_sums, entries, swap, *refs):
    slots, refs = refs[:count], refs[count:]
    own, refs = refs[:count], refs[count:]
    other, refs = refs[:count], refs[count:]
    sums, refs = refs[:n_sums], refs[n_sums:]
    (wa_ref, wb_ref, ga_ref, gb_ref), refs = refs[:4], refs[4:]
    (da_ref, db_ref, p_ref), refs = refs[:3], refs[3:]
    dq, refs = refs[:count], refs[count:]
    held, left, right, ah, al, bh, bl, dq_held, sem_q, sem_l, sem_r, sem_o = refs
    width = wb_ref.shape[0]
    for j in range(count):
        pltpu.make_async_copy(
            slots[j].at[:, 2 * width : 3 * width], held.at[j], sem_q.at[j]
        ).start()
        pltpu.make_async_copy(own[j], left.at[j], sem_l.at[j]).start()
        pltpu.make_async_copy(other[swap[j]], right.at[j], sem_r.at[j]).start()
    _, scale = scale_of(sums, entries)
    rate = inner_rate / scale
    ah[...], al[...] = halves(wa_ref[...].astype(f32) - ga_ref[...] * rate)
    bh[...], bl[...] = halves(wb_ref[...].astype(f32) - gb_ref[...] * rate)
    da_ref[...] = jnp.zeros_like(da_ref)
    db_ref[...] = jnp.zeros_like(db_ref)

    @pl.loop(0, count)
    def _(j):
        pltpu.make_async_copy(
            slots[0].at[:, 2 * width : 3 * width], held.at[j], sem_q.at[j]
        ).wait()
        pltpu.make_async_copy(own[0], left.at[j], sem_l.at[j]).wait()
        pltpu.make_async_copy(other[0], right.at[j], sem_r.at[j]).wait()
        queries = held[j]
        d_out = halves(left[j] + right[j])
        a = (ah[...], al[...])
        b = (bh[...], bl[...])
        mixed = two_right(nn, queries, a)
        u, w = mixed[:, :width], mixed[:, width:]
        sg = sigmoid(u)
        act = u * sg
        hb = three(nt, d_out, b)
        db_ref[...] += three(tn, halves(act * w), d_out)
        slope = sg * (1.0 + u * (1.0 - sg))
        ub = halves(hb * w * slope)
        wbar = halves(hb * act)
        da_ref[:, :width] += two_right(tn, queries, ub)
        da_ref[:, width:] += two_right(tn, queries, wbar)
        back = three(nt, ub, (ah[:, :width], al[:, :width])) + three(
            nt, wbar, (ah[:, width:], al[:, width:])
        )
        dq_held[j] = back.astype(bf16)

    copies = [pltpu.make_async_copy(dq_held.at[j], dq[j], sem_o.at[j]) for j in range(count)]
    for copy in copies:
        copy.start()
    total = jnp.sum(ga_ref[...] * da_ref[...]) + jnp.sum(gb_ref[...] * db_ref[...])
    p_ref[...] = jnp.zeros_like(p_ref) + total
    for copy in copies:
        copy.wait()


def call_query(slots, own, other, swap, sums, entries, wa, wb, ga, gb):
    count = len(slots)
    rows, width = slots[0].shape[0], wb.shape[0]
    outs = pl.pallas_call(
        partial(query_kernel, count, len(sums), entries, swap),
        out_shape=(shape_of(width, 2 * width), shape_of(width, width), shape_of(8, 128))
        + (shape_of(rows, width, dtype=bf16),) * count,
        in_specs=[any_spec()] * (3 * count) + [vmem_spec()] * (len(sums) + 4),
        out_specs=[vmem_spec()] * 3 + [any_spec()] * count,
        scratch_shapes=[
            pltpu.VMEM((count, rows, width), bf16),
            pltpu.VMEM((count, rows, width), f32),
            pltpu.VMEM((count, rows, width), f32),
            pltpu.VMEM((width, 2 * width), bf16),
            pltpu.VMEM((width, 2 * width), bf16),
            pltpu.VMEM((width, width), bf16),
            pltpu.VMEM((width, width), bf16),
            pltpu.VMEM((count, rows, width), bf16),
            pltpu.SemaphoreType.DMA((count,)),
            pltpu.SemaphoreType.DMA((count,)),
            pltpu.SemaphoreType.DMA((count,)),
            pltpu.SemaphoreType.DMA((count,)),
        ],
        compiler_params=pltpu.CompilerParams(vmem_limit_bytes=vmem_bytes),
        cost_estimate=estimate(20, rows * count),
        name="query_pull",
    )(*slots, *own, *other, *sums, wa, wb, ga, gb)
    return outs[0], outs[1], outs[2], outs[3:]


def key_kernel(count, n_sums, n_kept, entries, first, *refs):
    slots, refs = refs[:count], refs[count:]
    sums, refs = refs[:n_sums], refs[n_sums:]
    dots, refs = refs[:n_sums], refs[n_sums:]
    gain_ref, wa_ref, wb_ref, ga_ref, gb_ref, da_ref, db_ref = refs[:7]
    refs = refs[7:]
    kept, refs = refs[:n_kept], refs[n_kept:]
    out, refs = refs[:count], refs[count:]
    held, dah, dal, dbh, dbl, out_held, sem_k, sem_o = refs[:8]
    kept_held, kept_sems = refs[8 : 8 + n_kept], refs[8 + n_kept :]
    width = wb_ref.shape[0]
    fetch_all(slots, held, sem_k)
    for source, target, sems in zip(kept, kept_held, kept_sems):
        for j in range(count):
            pltpu.make_async_copy(source.at[first + j], target.at[j], sems.at[j]).start()
    gain = gain_ref[0]
    rms, scale = scale_of(sums, entries)
    product = dots[0][0:1, 0:1]
    for more in dots[1:]:
        product = product + more[0:1, 0:1]
    pull = product / (scale * scale * entries * rms)
    for d_ref, g_ref, h_ref, l_ref in (
        (da_ref, ga_ref, dah, dal),
        (db_ref, gb_ref, dbh, dbl),
    ):
        h_ref[...], l_ref[...] = halves(
            (d_ref[...] * (1.0 / scale) - g_ref[...] * pull) * (-inner_rate)
        )

    @pl.loop(0, count)
    def _(j):
        pltpu.make_async_copy(slots[0], held.at[j], sem_k.at[j]).wait()
        for source, target, sems in zip(kept, kept_held, kept_sems):
            pltpu.make_async_copy(source.at[first], target.at[j], sems.at[j]).wait()
        keys = held[j, :, :width]
        mixed = nn(keys, wa_ref[...]) * gain
        moved = two_right(nn, keys, (dah[...], dal[...])) * gain
        u, w = mixed[:, :width], mixed[:, width:]
        du, dw = moved[:, :width], moved[:, width:]
        sg = sigmoid(u)
        act = u * sg
        rest = 1.0 - sg
        slope = sg * (1.0 + u * rest)
        bend = sg * rest * (2.0 + u * (rest - sg))
        db = (dbh[...], dbl[...])
        hidden = halves(act * w)
        shift = two(nn, halves(slope * du * w + act * dw), wb_ref[...]) + three(nn, hidden, db)
        out_held[j, :, width:] = (-shift).astype(bf16)
        if n_kept:
            e2, hb = halves(kept_held[0][j]), kept_held[1][j]
        else:
            values = held[j, :, width : 2 * width].astype(f32)
            e2 = halves(two(nn, hidden, wb_ref[...]) - values)
            hb = two(nt, e2, wb_ref[...])
        back = two(nt, halves(shift), wb_ref[...]) + three(nt, e2, db)
        ub = halves(back * w * slope + hb * (bend * du * w + slope * dw))
        wbar = halves(back * act + hb * slope * du)
        ut = halves(hb * slope * w)
        wt = halves(hb * act)
        grad = (
            two(nt, ub, wa_ref[:, :width])
            + two(nt, wbar, wa_ref[:, width:])
            + three(nt, ut, (dah[:, :width], dal[:, :width]))
            + three(nt, wt, (dah[:, width:], dal[:, width:]))
        )
        out_held[j, :, :width] = (grad * gain).astype(bf16)

    copies = [pltpu.make_async_copy(out_held.at[j], out[j], sem_o.at[j]) for j in range(count)]
    for copy in copies:
        copy.start()
    for copy in copies:
        copy.wait()


def call_key(slots, sums, dots, entries, first, gain, wa, wb, ga, gb, da, db, *kept):
    count = len(slots)
    rows, width = slots[0].shape[0], wb.shape[0]
    return pl.pallas_call(
        partial(key_kernel, count, len(sums), len(kept), entries, first),
        out_shape=(shape_of(rows, 2 * width, dtype=bf16),) * count,
        in_specs=[any_spec()] * count
        + [vmem_spec()] * (2 * len(sums))
        + [smem_spec()]
        + [vmem_spec()] * 6
        + [any_spec()] * len(kept),
        out_specs=[any_spec()] * count,
        scratch_shapes=[
            pltpu.VMEM((count,) + slots[0].shape, bf16),
            pltpu.VMEM((width, 2 * width), bf16),
            pltpu.VMEM((width, 2 * width), bf16),
            pltpu.VMEM((width, width), bf16),
            pltpu.VMEM((width, width), bf16),
            pltpu.VMEM((count, rows, 2 * width), bf16),
            pltpu.SemaphoreType.DMA((count,)),
            pltpu.SemaphoreType.DMA((count,)),
        ]
        + [pltpu.VMEM((count, rows, width), f32)] * len(kept)
        + [pltpu.SemaphoreType.DMA((count,))] * len(kept),
        compiler_params=pltpu.CompilerParams(vmem_limit_bytes=vmem_bytes),
        cost_estimate=estimate(26, rows * count),
        name="key_pull",
    )(*slots, *sums, *dots, gain, wa, wb, ga, gb, da, db, *kept)


def per_device(queries, keys, values, fast_in, fast_out, key_gain, out_proj, grad_out):
    toks, heads = lax.axis_size("tok"), lax.axis_size("head")
    low, high = toks // 2 - 1, toks // 2
    width = fast_out.shape[1]
    entries = float(heads * (fast_in.shape[1] * fast_in.shape[2] + width * fast_out.shape[2]))
    wa, wb = fast_in[0], fast_out[0]
    place, head = lax.axis_index("tok"), lax.axis_index("head")
    core = lax.rem(head, 2)
    line = sorted(range(toks), key=lambda t: (abs(t - low), t))
    mirror = [toks - 1 - t for t in line]
    swap = tuple(mirror.index(t) for t in line)

    def root(h):
        return high if h % 2 else low

    def flat(t, h):
        return t * heads + h

    both = ("tok", "head")

    def to_root(j):
        return [(flat((mirror if h % 2 else line)[j], h), flat(root(h), h)) for h in range(heads)]

    def from_root(j):
        return [(b, a) for a, b in to_root(j)]

    rows_in = jnp.concatenate([keys, values, queries], axis=1)
    slots = [rows_in] + [lax.ppermute(rows_in, both, to_root(j)) for j in range(1, toks)]

    ga, gb, squares, *kept = call_inner_grad(slots, toks <= 8, key_gain, wa, wb)

    def exchange(value):
        across = [
            (flat(root(h), h), flat(root(h ^ 1), h ^ 1)) for h in range(heads)
        ]
        value = value + lax.ppermute(value, both, across)
        step = 2
        while step < heads:
            far = [(flat(root(h), h), flat(root(h), h ^ step)) for h in range(heads)]
            more = lax.ppermute(value, both, far)
            step *= 2
            if step < heads:
                value = value + more
            else:
                return value, more
        return (value,)

    sums = exchange(squares)

    blocks = [out_proj] + [
        lax.ppermute(out_proj, "tok", [(low - j, low), (high + j, high)])
        for j in range(1, toks // 2)
    ]
    quarter = grad_out.shape[1] // 4

    def side_of(parts):
        if len(parts) == 1:
            return parts[0]
        return jnp.where(
            place <= low, jnp.concatenate(parts[::-1], axis=1), jnp.concatenate(parts, axis=1)
        )

    near, far = side_of(blocks[: toks // 4]), side_of(blocks[toks // 4 :])
    w_mine = jnp.where(core == 0, near, far)
    w_theirs = jnp.where(core == 0, far, near)

    def columns(which, half_is_low):
        index = jnp.where(half_is_low, 1 - which, 2 + which)
        return lax.dynamic_slice_in_dim(grad_out, index * quarter, quarter, axis=1)

    def product(mine, theirs):
        return (
            lax.dot_general(mine, w_mine, (((1,), (1,)), ((), ())), preferred_element_type=f32)
            + lax.dot_general(
                theirs, w_theirs, (((1,), (1,)), ((), ())), preferred_element_type=f32
            )
        )

    cores = [(h, h ^ 1) for h in range(heads)]
    at_low = place <= low
    partials = [product(columns(core, at_low), columns(1 - core, at_low))]
    for j in range(1, toks):
        piece = lax.ppermute(
            columns(core, place == line[j]), "tok", [(line[j], low), (mirror[j], high)]
        )
        partials.append(product(piece, lax.ppermute(piece, "head", cores)))
    over = [
        (flat(high, h), flat(low, h)) if h % 2 == 0 else (flat(low, h), flat(high, h))
        for h in range(heads)
    ]
    others = [lax.ppermute(partial_sum, both, over) for partial_sum in partials]

    da, db, dots, dq = call_query(
        slots, partials, others, swap, sums, entries, wa, wb, ga, gb
    )
    dots = exchange(dots)
    is_root = place == jnp.where(core == 0, low, high)

    def home(slot_outs):
        back = None
        for j in range(1, toks):
            got = lax.ppermute(slot_outs[j], both, from_root(j))
            back = got if back is None else back + got
        return jnp.where(is_root, slot_outs[0], back)

    d_queries = home(dq)
    first = toks // 2
    outs_far = call_key(
        slots[first:], sums, dots, entries, first, key_gain, wa, wb, ga, gb, da, db, *kept
    )
    outs_near = call_key(
        slots[:first], sums, dots, entries, 0, key_gain, wa, wb, ga, gb, da, db, *kept
    )
    pair = home(list(outs_near) + list(outs_far))
    return d_queries, pair[:, :width], pair[:, width:]


def solution(mesh):
    rows = P(("groups", "tok"), "head")
    return jax.shard_map(
        per_device,
        mesh=mesh,
        in_specs=(
            rows,
            rows,
            rows,
            P("head", None, None),
            P("head", None, None),
            P("head"),
            P("head", "tok"),
            P(("groups", "tok"), None),
        ),
        out_specs=(rows, rows, rows),
        check_vma=False,
    )
```

time: 400 us -> 179 us (0.45)
  waiting for transfers between devices: 303 us -> 62.8 us
  Pallas kernels: 0 us -> 60.8 us
  starting transfers between devices: 0.12 us -> 35.3 us
  matrix products: 41.2 us -> 6.29 us
  between operations: 18.2 us -> 1.95 us
  blocking collectives: 15.1 us -> 0 us
  other arithmetic: 14.3 us -> 2.38 us
    psum x2 -> x0, waiting for transfers between devices: 241 us -> none  [the longest x1 121 us: per_device(): full_grad = lax.psum(partial_grad, 'tok')]
    ppermute x0 -> x24, waiting for transfers between devices: none -> 62.8 us  [the longest x6 34.5 us: home(): got = lax.ppermute(slot_outs[j], both, from_root(j))]
    all_gather x1 -> x0, waiting for transfers between devices: 61.2 us -> none  [per_device(): lax.all_gather(out_proj, 'tok', axis=1, tiled=True)]
    pallas_call x0 -> x4, Pallas kernels: none -> 60.8 us  [the longest x2 28.8 us: call_key(): pl.pallas_call(partial(key_kernel, count, len(sums), len(kept), entries,...]
    ppermute x0 -> x24, starting transfers between devices: none -> 35.3 us  [the longest x3 7.6 us: per_device(): lax.ppermute(rows_in, both, to_root(j))]
    dot_general x18 -> x8, matrix products: 41.2 us -> 6.29 us  [the longest x4 4.38 us: product(): lax.dot_general(mine, w_mine, (((1,), (1,)), ((), ())), preferred_element...]
    psum x2 -> x0, blocking collectives: 15.1 us -> none  [the longest x1 7.58 us: per_device(): product = lax.psum(frobenius(full_grad, adjoint), 'head')]
    reduce_sum x4 -> x0, other arithmetic: 10.1 us -> none  [frobenius(): return jnp.sum(former[0] * latter[0]) + jnp.sum(former[1] * latter[1])]
  transfers between devices with their start and end apart: 3 -> 24, of which waited for: 3 -> 3; matrix products, arithmetic and copies ran while one was open for 3% -> 7% of each run, Pallas kernels for 0% -> 23%
where the time goes in v1:
time: 179 us; the launch traced here: 178 us
  waiting for transfers between devices  62.8 us (35%)
  Pallas kernels  60.8 us (34%)
  starting transfers between devices  35.3 us (20%)
  local copies, waits for them, and re-layouts  8.81 us (5%)
  matrix products  6.29 us (4%)
  other arithmetic  2.38 us (1%)
  between operations  1.95 us (1%)
    ppermute x6, waiting for transfers between devices, home(): got = lax.ppermute(slot_outs[j], both, from_root(j))  34.5 us
    pallas_call x2, Pallas kernels, call_key(): pl.pallas_call(partial(key_kernel, count, len(sums), len(kept), entries,...  28.8 us
    ppermute x3, waiting for transfers between devices, per_device(): lax.ppermute(columns(core, place == line[j]), 'tok', [(line[j], low), (mi...  28.3 us
    pallas_call x1, Pallas kernels, call_query(): pl.pallas_call(partial(query_kernel, count, len(sums), entries, swap), ou...  19 us
    pallas_call x1, Pallas kernels, call_inner_grad(): pl.pallas_call(partial(inner_grad_kernel, count, keep), out_shape=(shape_...  13 us
    ppermute x3, starting transfers between devices, per_device(): lax.ppermute(rows_in, both, to_root(j))  7.6 us
    ppermute x3, starting transfers between devices, per_device(): lax.ppermute(columns(core, place == line[j]), 'tok', [(line[j], low), (mi...  6 us
    ppermute x6, starting transfers between devices, home(): got = lax.ppermute(slot_outs[j], both, from_root(j))  5.68 us
  transfers between devices with their start and end apart: 24, of which 3 were waited for; matrix products, arithmetic and copies ran while one was open for 7% of the time, Pallas kernels for 23%

profile of v1, /device:TPU:0, one launch (start us, length us, event | category | flops | bytes accessed | tf_op | source)
XLA Modules:
  0.0 178.3 jit_solution(10285357757605875242)
XLA Ops:
  0.6 5.1 %collective-permute-start.3 = (bf16[512,1024]{1,0:T(8,128)(2,1)}, bf16[512,1024]{1,0:T(8,128)(2,1)S(1)}, u32[]{:S(2)}, u32[]{:S(2)}) collective-permute-start(bf16[512,1024]{1,0:T(8,128)(2,1)} %param.14), channel_id=1, source_target_pairs={{0,4},{12,8},{1,5},{13,9},{2,6},{14,10},{3,7},{15,11},{16,20},{28,... | collective-permute-start | bytes 3145736 | tf_op jit(solution)/shard_map/ppermute | solution.py:387
  5.8 2.4 %constant_dynamic-slice_fusion = (bf16[256,1024]{1,0:T(8,128)(2,1)}, bf16[256,1024]{1,0:T(8,128)(2,1)S(1)}, bf16[256,1024]{1,0:T(8,128)(2,1)S(1)}) fusion(bf16[256,4096]{1,0:T(8,128)(2,1)} %param.15, s32[]{:T(128)S(6)} %select_n.77, s32[]{:T(128)S(6)} %select_n.73, s32[]{:T(128)S(6)} %select_n.75), kind=kLoop, calls=%fused_computation.14 | loop fusion | bytes 3145740 | tf_op jit(solution)/shard_map/dynamic_slice | solution.py:405
  8.2 3.1 %collective-permute-start.8 = (bf16[256,1024]{1,0:T(8,128)(2,1)}, bf16[256,1024]{1,0:T(8,128)(2,1)}, u32[]{:S(2)}, u32[]{:S(2)}) collective-permute-start(bf16[256,1024]{1,0:T(8,128)(2,1)} %get-tuple-element.35), channel_id=1, source_target_pairs={{12,4},{0,8},{13,5},{1,9},{14,6},{2,10},{15,7},{3,11},{28,20},{16,... | collective-permute-start | bytes 1572872 | tf_op jit(solution)/shard_map/ppermute | solution.py:419
  11.3 0.7 constant_dynamic-update-slice_fusion.2
  12.0 0.8 constant_dynamic-update-slice_fusion.1
  12.8 0.7 constant_dynamic-update-slice_fusion.refs_0_
  13.5 1.6 collective-permute-start.2
  15.1 1.5 collective-permute-start.1
  16.6 2.1 %collective-permute-start.4 = (bf16[256,1024]{1,0:T(8,128)(2,1)S(1)}, bf16[256,1024]{1,0:T(8,128)(2,1)}, u32[]{:S(2)}, u32[]{:S(2)}) collective-permute-start(bf16[256,1024]{1,0:T(8,128)(2,1)S(1)} %get-tuple-element.36), channel_id=1, source_target_pairs={{0,4},{12,8},{1,5},{13,9},{2,6},{14,10},{3,7},{15,11},{16,20},{28,... | collective-permute-start | bytes 1572872 | tf_op jit(solution)/shard_map/ppermute | solution.py:419
  19.4 21.4 %collective-permute-done.8 = bf16[256,1024]{1,0:T(8,128)(2,1)} collective-permute-done((bf16[256,1024]{1,0:T(8,128)(2,1)}, bf16[256,1024]{1,0:T(8,128)(2,1)}, u32[]{:S(2)}, u32[]{:S(2)}) %collective-permute-start.8) | collective-permute-done | bytes 524320 | tf_op jit(solution)/shard_map/ppermute | solution.py:419
  40.8 0.8 collective-permute-start.6
  41.6 0.0 collective-permute-done.3
  41.6 0.1 collective-permute-start.9
  41.7 0.1 broadcast_select_fusion.1
  41.9 0.5 copy-done
  42.4 0.5 fusion
  42.9 0.5 convolution_add_fusion.3.refs_4_
  43.4 1.7 fusion.8
  45.1 6.8 %collective-permute-done.4 = bf16[256,1024]{1,0:T(8,128)(2,1)} collective-permute-done((bf16[256,1024]{1,0:T(8,128)(2,1)S(1)}, bf16[256,1024]{1,0:T(8,128)(2,1)}, u32[]{:S(2)}, u32[]{:S(2)}) %collective-permute-start.4) | collective-permute-done | bytes 524320 | tf_op jit(solution)/shard_map/ppermute | solution.py:419
  51.9 4.5 %collective-permute-start = (bf16[256,1536]{1,0:T(8,128)(2,1)}, bf16[256,1536]{1,0:T(8,128)(2,1)S(1)}, u32[]{:S(2)}, u32[]{:S(2)}) collective-permute-start(bf16[256,1536]{1,0:T(8,128)(2,1)} %constant_dynamic-update-slice_fusion.refs_0_), channel_id=1, source_target_pairs={{0,4},{13,9},{2,6},{15,11},{16,20},{29,25},{18,22},{31,27}} | collective-permute-start | bytes 2359304 | tf_op jit(solution)/shard_map/ppermute | solution.py:364
  56.5 5.2 %collective-permute-start.5 = (bf16[256,1024]{1,0:T(8,128)(2,1)}, bf16[256,1024]{1,0:T(8,128)(2,1)S(1)}, u32[]{:S(2)}, u32[]{:S(2)}) collective-permute-start(bf16[256,1024]{1,0:T(8,128)(2,1)} %collective-permute-done.4), channel_id=1, source_target_pairs={{0,1},{1,0},{2,3},{3,2},{4,5},{5,4},{6,7},{7,6},{8,9},{9,8},{10,11... | collective-permute-start | bytes 1572872 | tf_op jit(solution)/shard_map/ppermute | solution.py:422
  61.7 0.1 collective-permute-start.7
  61.7 0.5 convolution_add_fusion.refs_7_
  62.2 1.7 fusion.6
  64.0 0.5 fusion.7
  64.4 0.0 collective-permute-done.5
  64.5 0.7 collective-permute-start.10
  65.2 0.5 convolution_add_fusion.2.refs_5_
  65.7 0.0 collective-permute-done.7
  65.7 0.7 collective-permute-start.13
  66.4 0.5 convolution_add_fusion.1.refs_6_
  66.9 0.0 collective-permute-done.2.refs_3_.refs_1_
  66.9 0.7 collective-permute-start.11
  67.6 0.7 collective-permute-start.12
  68.3 0.0 collective-permute-done.refs_1_
  68.3 0.9 copy-done.12
  69.3 13.0 %inner_grad.1 = (f32[512,1024]{1,0:T(8,128)}, f32[512,512]{1,0:T(8,128)}, f32[8,128]{1,0:T(8,128)}, f32[4,256,512]{2,1,0:T(8,128)}, f32[4,256,512]{2,1,0:T(8,128)}) custom-call(bf16[256,1536]{1,0:T(8,128)(2,1)} %constant_dynamic-update-slice_fusion.refs_0_, bf16[256,1536]{1,0:T(8,128)(2,1)} %copy-done.12, ...), custom_call_target="tpu_custom_call" | custom-call | flops 6979321856 | bytes 8388608 | tf_op jit(solution)/shard_map/inner_grad/pallas_call | solution.py:120
  82.3 0.7 collective-permute-start.14
  83.0 0.7 add.66.refs_12_.refs_2_
  83.7 0.8 collective-permute-start.15
  84.6 0.5 copy-done.19
  85.1 0.2 copy-done.13
  85.4 0.2 copy-done.14
  85.6 0.2 copy-done.15
  85.7 0.2 copy-done.16
  85.9 19.0 %query_pull.1 = (f32[512,1024]{1,0:T(8,128)}, f32[512,512]{1,0:T(8,128)}, f32[8,128]{1,0:T(8,128)}, bf16[256,512]{1,0:T(8,128)(2,1)}, bf16[256,512]{1,0:T(8,128)...) custom-call(bf16[256,1536]{1,0:T(8,128)(2,1)} %constant_dynamic-update-slice_fusion.refs_0_, ...), custom_call_target="tpu_custom_call" | custom-call | flops 10737418240 | bytes 8388608 | tf_op jit(solution)/shard_map/query_pull/pallas_call | solution.py:206
  104.9 0.7 collective-permute-start.19
  105.5 0.7 add.69.refs_4_
  106.2 0.6 collective-permute-start.20
  106.9 1.3 collective-permute-start.16
  108.2 0.6 copy-done.20
  108.8 14.4 %key_pull.3 = (bf16[256,1024]{1,0:T(8,128)(2,1)}, bf16[256,1024]{1,0:T(8,128)(2,1)}) custom-call(bf16[256,1536]{1,0:T(8,128)(2,1)} %collective-permute-done.1.refs_2_.refs_0_, bf16[256,1536]{1,0:T(8,128)(2,1)} %collective-permute-done.2.refs_3_.refs_1_, f32[8,128]{1,0:T(8,128)} %copy-done.10, f32[8,128]{1,0:T(8,128)} %copy-done.19, f32[8,128]{1,0:T(8,128)} %copy-done.11, ...), custom_call_target="tpu_custom_call" | custom-call | flops 6979321856 | bytes 8388608 | tf_op jit(solution)/shard_map/key_pull/pallas_call | solution.py:310
  123.2 0.7 collective-permute-start.22
  123.9 0.0 copy-start.18
  123.9 0.0 copy-start.6
  123.9 1.0 collective-permute-start.23
  125.0 14.4 %key_pull.2 = (bf16[256,1024]{1,0:T(8,128)(2,1)}, bf16[256,1024]{1,0:T(8,128)(2,1)}) custom-call(bf16[256,1536]{1,0:T(8,128)(2,1)} %constant_dynamic-update-slice_fusion.refs_0_, bf16[256,1536]{1,0:T(8,128)(2,1)} %copy-done.12, f32[8,128]{1,0:T(8,128)} %copy-done.10, f32[8,128]{1,0:T(8,128)} %copy-done.19, f32[8,128]{1,0:T(8,128)} %copy-done.11, ...), custom_call_target="tpu_custom_call" | custom-call | flops 6979321856 | bytes 8388608 | tf_op jit(solution)/shard_map/key_pull/pallas_call | solution.py:310
  139.4 1.3 collective-permute-start.21
  140.7 0.7 collective-permute-start.17
  141.4 0.7 collective-permute-start.18
  142.2 0.8 add_select_fusion.1
  142.9 34.5 %collective-permute-done.21 = bf16[256,1024]{1,0:T(8,128)(2,1)S(1)} collective-permute-done((bf16[256,1024]{1,0:T(8,128)(2,1)}, bf16[256,1024]{1,0:T(8,128)(2,1)S(1)}, u32[]{:S(2)}, u32[]{:S(2)}) %collective-permute-start.21) | collective-permute-done | bytes 524320 | tf_op jit(solution)/shard_map/ppermute | solution.py:438
  177.4 0.1 add_select_fusion
  177.5 0.8 fusion.5
  (48 shorter events, 0.1 us)
Async XLA Ops:
  0.6 10.7 %copy-start.7 = (bf16[256,512]{1,0:T(8,128)(2,1)S(1)}, bf16[256,512]{1,0:T(8,128)(2,1)}, u32[]{:S(2)}) copy-start(bf16[256,512]{1,0:T(8,128)(2,1)} %param.9) | copy-start | bytes 786436
  0.6 41.0 %collective-permute-start.3 = (bf16[512,1024]{1,0:T(8,128)(2,1)}, bf16[512,1024]{1,0:T(8,128)(2,1)S(1)}, u32[]{:S(2)}, u32[]{:S(2)}) collective-permute-start(bf16[512,1024]{1,0:T(8,128)(2,1)} %param.14), channel_id=1, source_target_pairs={{0,4},{12,8},{1,5},{13,9},{2,6},{14,10},{3,7},{15,11},{16,20},{28,... | collective-permute-start | bytes 3145736 | tf_op jit(solution)/shard_map/ppermute | solution.py:387
  5.8 6.2 %copy-start.8 = (bf16[256,512]{1,0:T(8,128)(2,1)S(1)}, bf16[256,512]{1,0:T(8,128)(2,1)}, u32[]{:S(2)}) copy-start(bf16[256,512]{1,0:T(8,128)(2,1)} %param.10) | copy-start | bytes 786436
  5.8 7.0 %copy-start.9 = (bf16[256,512]{1,0:T(8,128)(2,1)S(1)}, bf16[256,512]{1,0:T(8,128)(2,1)}, u32[]{:S(2)}) copy-start(bf16[256,512]{1,0:T(8,128)(2,1)} %param.8) | copy-start | bytes 786436
  5.8 35.9 %copy-start.1 = (bf16[512,1024]{1,0:T(8,128)(2,1)S(1)}, bf16[512,1024]{1,0:T(8,128)(2,1)}, u32[]{:S(2)}) copy-start(bf16[512,1024]{1,0:T(8,128)(2,1)} %param.14) | copy-start | bytes 3145732
  8.2 32.6 %collective-permute-start.8 = (bf16[256,1024]{1,0:T(8,128)(2,1)}, bf16[256,1024]{1,0:T(8,128)(2,1)}, u32[]{:S(2)}, u32[]{:S(2)}) collective-permute-start(bf16[256,1024]{1,0:T(8,128)(2,1)} %get-tuple-element.35), channel_id=1, source_target_pairs={{12,4},{0,8},{13,5},{1,9},{14,6},{2,10},{15,7},{3,11},{28,20},{16,... | collective-permute-start | bytes 1572872 | tf_op jit(solution)/shard_map/ppermute | solution.py:419
  13.5 53.4 %collective-permute-start.2 = (bf16[256,1536]{1,0:T(8,128)(2,1)}, bf16[256,1536]{1,0:T(8,128)(2,1)}, u32[]{:S(2)}, u32[]{:S(2)}) collective-permute-start(bf16[256,1536]{1,0:T(8,128)(2,1)} %constant_dynamic-update-slice_fusion.refs_0_), channel_id=1, source_target_pairs={{12,4},{1,9},{14,6},{3,11},{28,20},{17,25},{30,22},{19,27}} | collective-permute-start | bytes 2359304 | tf_op jit(solution)/shard_map/ppermute | solution.py:364
  15.1 52.5 %collective-permute-start.1 = (bf16[256,1536]{1,0:T(8,128)(2,1)}, bf16[256,1536]{1,0:T(8,128)(2,1)}, u32[]{:S(2)}, u32[]{:S(2)}) collective-permute-start(bf16[256,1536]{1,0:T(8,128)(2,1)} %constant_dynamic-update-slice_fusion.refs_0_), channel_id=1, source_target_pairs={{8,4},{5,9},{10,6},{7,11},{24,20},{21,25},{26,22},{23,27}} | collective-permute-start | bytes 2359304 | tf_op jit(solution)/shard_map/ppermute | solution.py:364
  16.6 35.3 %collective-permute-start.4 = (bf16[256,1024]{1,0:T(8,128)(2,1)S(1)}, bf16[256,1024]{1,0:T(8,128)(2,1)}, u32[]{:S(2)}, u32[]{:S(2)}) collective-permute-start(bf16[256,1024]{1,0:T(8,128)(2,1)S(1)} %get-tuple-element.36), channel_id=1, source_target_pairs={{0,4},{12,8},{1,5},{13,9},{2,6},{14,10},{3,7},{15,11},{16,20},{28,... | collective-permute-start | bytes 1572872 | tf_op jit(solution)/shard_map/ppermute | solution.py:419
  40.8 1.6 copy-start
  40.8 15.7 %collective-permute-start.6 = (bf16[256,1024]{1,0:T(8,128)(2,1)S(1)}, bf16[256,1024]{1,0:T(8,128)(2,1)S(1)}, u32[]{:S(2)}, u32[]{:S(2)}) collective-permute-start(bf16[256,1024]{1,0:T(8,128)(2,1)S(1)} %get-tuple-element.37), channel_id=1, source_target_pairs={{8,4},{4,8},{9,5},{5,9},{10,6},{6,10},{11,7},{7,11},{24,20},{20,24... | collective-permute-start | bytes 1572872 | tf_op jit(solution)/shard_map/ppermute | solution.py:419
  41.6 20.0 %collective-permute-start.9 = (bf16[256,1024]{1,0:T(8,128)(2,1)}, bf16[256,1024]{1,0:T(8,128)(2,1)S(1)}, u32[]{:S(2)}, u32[]{:S(2)}) collective-permute-start(bf16[256,1024]{1,0:T(8,128)(2,1)} %collective-permute-done.8), channel_id=1, source_target_pairs={{0,1},{1,0},{2,3},{3,2},{4,5},{5,4},{6,7},{7,6},{8,9},{9,8},{10,11... | collective-permute-start | bytes 1572872 | tf_op jit(solution)/shard_map/ppermute | solution.py:422
  43.4 21.1 %copy-start.5 = (f32[256,512]{1,0:T(8,128)}, f32[256,512]{1,0:T(8,128)S(1)}, u32[]{:S(2)}) copy-start(f32[256,512]{1,0:T(8,128)S(1)} %convolution_add_fusion.3.refs_4_) | copy-start | bytes 1572868
  51.9 16.4 %collective-permute-start = (bf16[256,1536]{1,0:T(8,128)(2,1)}, bf16[256,1536]{1,0:T(8,128)(2,1)S(1)}, u32[]{:S(2)}, u32[]{:S(2)}) collective-permute-start(bf16[256,1536]{1,0:T(8,128)(2,1)} %constant_dynamic-update-slice_fusion.refs_0_), channel_id=1, source_target_pairs={{0,4},{13,9},{2,6},{15,11},{16,20},{29,25},{18,22},{31,27}} | collective-permute-start | bytes 2359304 | tf_op jit(solution)/shard_map/ppermute | solution.py:364
  56.5 8.0 %collective-permute-start.5 = (bf16[256,1024]{1,0:T(8,128)(2,1)}, bf16[256,1024]{1,0:T(8,128)(2,1)S(1)}, u32[]{:S(2)}, u32[]{:S(2)}) collective-permute-start(bf16[256,1024]{1,0:T(8,128)(2,1)} %collective-permute-done.4), channel_id=1, source_target_pairs={{0,1},{1,0},{2,3},{3,2},{4,5},{5,4},{6,7},{7,6},{8,9},{9,8},{10,11... | collective-permute-start | bytes 1572872 | tf_op jit(solution)/shard_map/ppermute | solution.py:422
  61.7 4.0 %collective-permute-start.7 = (bf16[256,1024]{1,0:T(8,128)(2,1)S(1)}, bf16[256,1024]{1,0:T(8,128)(2,1)S(1)}, u32[]{:S(2)}, u32[]{:S(2)}) collective-permute-start(bf16[256,1024]{1,0:T(8,128)(2,1)S(1)} %collective-permute-done.6), channel_id=1, source_target_pairs={{0,1},{1,0},{2,3},{3,2},{4,5},{5,4},{6,7},{7,6},{8,9},{9,8},{10,11... | collective-permute-start | bytes 1572872 | tf_op jit(solution)/shard_map/ppermute | solution.py:422
  62.2 3.4 %copy-start.2 = (f32[256,512]{1,0:T(8,128)}, f32[256,512]{1,0:T(8,128)S(1)}, u32[]{:S(2)}) copy-start(f32[256,512]{1,0:T(8,128)S(1)} %convolution_add_fusion.refs_7_) | copy-start | bytes 1572868
  64.5 20.1 %collective-permute-start.10 = (f32[256,512]{1,0:T(8,128)S(1)}, f32[256,512]{1,0:T(8,128)S(1)}, u32[]{:S(2)}, u32[]{:S(2)}) collective-permute-start(f32[256,512]{1,0:T(8,128)S(1)} %convolution_add_fusion.3.refs_4_), channel_id=1, source_target_pairs={{8,4},{5,9},{10,6},{7,11},{24,20},{21,25},{26,22},{23,27}} | collective-permute-start | bytes 1572872 | tf_op jit(solution)/shard_map/ppermute | solution.py:427
  65.7 16.6 %copy-start.3 = (f32[256,512]{1,0:T(8,128)}, f32[256,512]{1,0:T(8,128)S(1)}, u32[]{:S(2)}) copy-start(f32[256,512]{1,0:T(8,128)S(1)} %convolution_add_fusion.2.refs_5_) | copy-start | bytes 1572868
  65.7 18.9 %collective-permute-start.13 = (f32[256,512]{1,0:T(8,128)S(1)}, f32[256,512]{1,0:T(8,128)S(1)}, u32[]{:S(2)}, u32[]{:S(2)}) collective-permute-start(f32[256,512]{1,0:T(8,128)S(1)} %convolution_add_fusion.refs_7_), channel_id=1, source_target_pairs={{8,4},{5,9},{10,6},{7,11},{24,20},{21,25},{26,22},{23,27}} | collective-permute-start | bytes 1572872 | tf_op jit(solution)/shard_map/ppermute | solution.py:427
  66.9 15.4 %copy-start.4 = (f32[256,512]{1,0:T(8,128)}, f32[256,512]{1,0:T(8,128)S(1)}, u32[]{:S(2)}) copy-start(f32[256,512]{1,0:T(8,128)S(1)} %convolution_add_fusion.1.refs_6_) | copy-start | bytes 1572868
  66.9 17.7 %collective-permute-start.11 = (f32[256,512]{1,0:T(8,128)S(1)}, f32[256,512]{1,0:T(8,128)S(1)}, u32[]{:S(2)}, u32[]{:S(2)}) collective-permute-start(f32[256,512]{1,0:T(8,128)S(1)} %convolution_add_fusion.2.refs_5_), channel_id=1, source_target_pairs={{8,4},{5,9},{10,6},{7,11},{24,20},{21,25},{26,22},{23,27}} | collective-permute-start | bytes 1572872 | tf_op jit(solution)/shard_map/ppermute | solution.py:427
  67.6 17.0 %collective-permute-start.12 = (f32[256,512]{1,0:T(8,128)S(1)}, f32[256,512]{1,0:T(8,128)S(1)}, u32[]{:S(2)}, u32[]{:S(2)}) collective-permute-start(f32[256,512]{1,0:T(8,128)S(1)} %convolution_add_fusion.1.refs_6_), channel_id=1, source_target_pairs={{8,4},{5,9},{10,6},{7,11},{24,20},{21,25},{26,22},{23,27}} | collective-permute-start | bytes 1572872 | tf_op jit(solution)/shard_map/ppermute | solution.py:427
  68.3 1.0 copy-start.12
  82.3 0.7 collective-permute-start.14
  83.7 0.9 copy-start.10
  83.7 0.8 collective-permute-start.15
  84.5 0.6 copy-start.19
  84.5 0.8 copy-start.13
  84.6 1.0 copy-start.14
  84.6 1.1 copy-start.15
  84.6 1.3 copy-start.16
  104.9 0.7 collective-permute-start.19
  106.2 2.0 %copy-start.11 = (f32[8,128]{1,0:T(8,128)}, f32[8,128]{1,0:T(8,128)S(1)}, u32[]{:S(2)}) copy-start(f32[8,128]{1,0:T(8,128)S(1)} %add.69.refs_4_) | copy-start | bytes 12292
  106.2 2.0 %collective-permute-start.20 = (f32[8,128]{1,0:T(8,128)S(1)}, f32[8,128]{1,0:T(8,128)S(1)}, u32[]{:S(2)}, u32[]{:S(2)}) collective-permute-start(f32[8,128]{1,0:T(8,128)S(1)} %add.69.refs_4_), channel_id=1, source_target_pairs={{4,6},{9,11},{6,4},{11,9},{20,22},{25,27},{22,20},{27,25}} | collective-permute-start | bytes 12296 | tf_op jit(solution)/shard_map/ppermute | solution.py:376
  106.9 34.5 %collective-permute-start.16 = (bf16[256,512]{1,0:T(8,128)(2,1)}, bf16[256,512]{1,0:T(8,128)(2,1)S(1)}, u32[]{:S(2)}, u32[]{:S(2)}) collective-permute-start(bf16[256,512]{1,0:T(8,128)(2,1)} %get-tuple-element.23), channel_id=1, source_target_pairs={{4,0},{9,13},{6,2},{11,15},{20,16},{25,29},{22,18},{27,31}} | collective-permute-start | bytes 786440 | tf_op jit(solution)/shard_map/ppermute | solution.py:438
  108.2 0.6 copy-start.20
  123.2 19.7 %collective-permute-start.22 = (bf16[256,1024]{1,0:T(8,128)(2,1)}, bf16[256,1024]{1,0:T(8,128)(2,1)S(1)}, u32[]{:S(2)}, u32[]{:S(2)}) collective-permute-start(bf16[256,1024]{1,0:T(8,128)(2,1)} %get-tuple-element.33), channel_id=1, source_target_pairs={{4,8},{9,5},{6,10},{11,7},{20,24},{25,21},{22,26},{27,23}} | collective-permute-start | bytes 1572872 | tf_op jit(solution)/shard_map/ppermute | solution.py:438
  123.9 16.8 %copy-start.18 = (bf16[256,512]{1,0:T(8,128)(2,1)S(1)}, bf16[256,512]{1,0:T(8,128)(2,1)}, u32[]{:S(2)}) copy-start(bf16[256,512]{1,0:T(8,128)(2,1)} %get-tuple-element.24) | copy-start | bytes 786436
  123.9 17.5 %copy-start.17 = (bf16[256,512]{1,0:T(8,128)(2,1)S(1)}, bf16[256,512]{1,0:T(8,128)(2,1)}, u32[]{:S(2)}) copy-start(bf16[256,512]{1,0:T(8,128)(2,1)} %get-tuple-element.25) | copy-start | bytes 786436
  123.9 18.2 %copy-start.6 = (bf16[256,512]{1,0:T(8,128)(2,1)S(1)}, bf16[256,512]{1,0:T(8,128)(2,1)}, u32[]{:S(2)}) copy-start(bf16[256,512]{1,0:T(8,128)(2,1)} %get-tuple-element.22) | copy-start | bytes 786436
  123.9 19.0 %collective-permute-start.23 = (bf16[256,1024]{1,0:T(8,128)(2,1)}, bf16[256,1024]{1,0:T(8,128)(2,1)S(1)}, u32[]{:S(2)}, u32[]{:S(2)}) collective-permute-start(bf16[256,1024]{1,0:T(8,128)(2,1)} %get-tuple-element.34), channel_id=1, source_target_pairs={{4,12},{9,1},{6,14},{11,3},{20,28},{25,17},{22,30},{27,19}} | collective-permute-start | bytes 1572872 | tf_op jit(solution)/shard_map/ppermute | solution.py:438
  139.4 38.0 %collective-permute-start.21 = (bf16[256,1024]{1,0:T(8,128)(2,1)}, bf16[256,1024]{1,0:T(8,128)(2,1)S(1)}, u32[]{:S(2)}, u32[]{:S(2)}) collective-permute-start(bf16[256,1024]{1,0:T(8,128)(2,1)} %get-tuple-element.32), channel_id=1, source_target_pairs={{4,0},{9,13},{6,2},{11,15},{20,16},{25,29},{22,18},{27,31}} | collective-permute-start | bytes 1572872 | tf_op jit(solution)/shard_map/ppermute | solution.py:438
  140.7 1.4 collective-permute-start.17
  141.4 0.7 collective-permute-start.18

commit v2 on v1

--- a/solution.py
+++ b/solution.py
@@ -13,6 +13,7 @@
 norm_eps = 1e-06
 vmem_bytes = 56 * 1024 * 1024
 MIB = 1024 * 1024
+JOIN = 1
 
 
 def halves(x):
@@ -32,42 +33,68 @@
     return lax.dot_general(a, b, (((0,), (0,)), ((), ())), preferred_element_type=f32)
 
 
+def joined(dot, a, b):
+    left, right = {nn: (1, 0), nt: (1, 1), tn: (0, 0)}[dot]
+    return dot(jnp.concatenate(a, axis=left), jnp.concatenate(b, axis=right))
+
+
 def two(dot, a, b):
-    return dot(a[0], b) + dot(a[1], b)
+    return joined(dot, a, (b, b))
 
 
 def two_right(dot, a, b):
-    return dot(a, b[0]) + dot(a, b[1])
+    return joined(dot, (a, a), b)
 
 
 def three(dot, a, b):
-    return dot(a[0], b[0]) + dot(a[0], b[1]) + dot(a[1], b[0])
+    return joined(dot, (a[0], a[0], a[1]), (b[0], b[1], b[0]))
 
 
 def sigmoid(u):
     return 1.0 / (1.0 + jnp.exp(-u))
 
 
-def fetch_all(slots, held, sems):
-    for j, slot in enumerate(slots):
-        pltpu.make_async_copy(slot, held.at[j], sems.at[j]).start()
+def part(j, rows):
+    return pl.ds(pl.multiple_of(j * rows, rows), rows)
+
+
+def fetch(sources, held, sems):
+    rows = held.shape[0] // len(sources)
+    for j, source in enumerate(sources):
+        pltpu.make_async_copy(source, held.at[part(j, rows)], sems.at[j]).start()
+
+    def wait(j):
+        pltpu.make_async_copy(sources[0], held.at[part(j, rows)], sems.at[j]).wait()
+
+    return wait
+
+
+def joined_loop(count, rows, waits, body):
+    join = JOIN
+    while count % join:
+        join -= 1
+
+    @pl.loop(0, count // join)
+    def _(i):
+        for wait in waits:
+            for k in range(join):
+                wait(i * join + k)
+        body(part(i, rows * join))
 
 
 def inner_grad_kernel(count, keep, *refs):
     slots = refs[:count]
     gain_ref, wa_ref, wb_ref, ga_ref, gb_ref, sq_ref = refs[count : count + 6]
     held, sems = refs[-2:]
-    fetch_all(slots, held, sems)
+    wait = fetch(slots, held, sems)
     gain = gain_ref[0]
     width = wb_ref.shape[0]
     ga_ref[...] = jnp.zeros_like(ga_ref)
     gb_ref[...] = jnp.zeros_like(gb_ref)
 
-    @pl.loop(0, count)
-    def _(j):
-        pltpu.make_async_copy(slots[0], held.at[j], sems.at[j]).wait()
-        keys = held[j, :, :width]
-        values = held[j, :, width : 2 * width].astype(f32)
+    def body(j):
+        keys = held[j, :width]
+        values = held[j, width : 2 * width].astype(f32)
         mixed = nn(keys, wa_ref[...]) * gain
         u, w = mixed[:, :width], mixed[:, width:]
         sg = sigmoid(u)
@@ -85,6 +112,7 @@
         ga_ref[:, :width] += two_right(tn, keys, halves(hb * w * slope))
         ga_ref[:, width:] += two_right(tn, keys, halves(hb * act))
 
+    joined_loop(count, slots[0].shape[0], [wait], body)
     ga = ga_ref[...] * gain
     ga_ref[...] = ga
     gb = gb_ref[...]
@@ -109,7 +137,7 @@
 
 def estimate(units, rows):
     return pl.CostEstimate(
-        flops=units * 2 * rows * 512 * 512, bytes_accessed=8 * MIB, transcendentals=0
+        flops=int(units * 2 * rows * 512 * 512), bytes_accessed=MIB, transcendentals=0
     )
 
 
@@ -120,11 +148,11 @@
     return pl.pallas_call(
         partial(inner_grad_kernel, count, keep),
         out_shape=(shape_of(width, 2 * width), shape_of(width, width), shape_of(8, 128))
-        + (shape_of(count, rows, width),) * kept,
+        + (shape_of(count * rows, width),) * kept,
         in_specs=[any_spec()] * count + [smem_spec(), vmem_spec(), vmem_spec()],
         out_specs=[vmem_spec()] * (3 + kept),
         scratch_shapes=[
-            pltpu.VMEM((count,) + slots[0].shape, bf16),
+            pltpu.VMEM((count * rows, slots[0].shape[1]), bf16),
             pltpu.SemaphoreType.DMA((count,)),
         ],
         compiler_params=pltpu.CompilerParams(vmem_limit_bytes=vmem_bytes),
@@ -151,12 +179,11 @@
     dq, refs = refs[:count], refs[count:]
     held, left, right, ah, al, bh, bl, dq_held, sem_q, sem_l, sem_r, sem_o = refs
     width = wb_ref.shape[0]
-    for j in range(count):
-        pltpu.make_async_copy(
-            slots[j].at[:, 2 * width : 3 * width], held.at[j], sem_q.at[j]
-        ).start()
-        pltpu.make_async_copy(own[j], left.at[j], sem_l.at[j]).start()
-        pltpu.make_async_copy(other[swap[j]], right.at[j], sem_r.at[j]).start()
+    waits = [
+        fetch([slot.at[:, 2 * width : 3 * width] for slot in slots], held, sem_q),
+        fetch(own, left, sem_l),
+        fetch([other[swap[j]] for j in range(count)], right, sem_r),
+    ]
     _, scale = scale_of(sums, entries)
     rate = inner_rate / scale
     ah[...], al[...] = halves(wa_ref[...].astype(f32) - ga_ref[...] * rate)
@@ -164,13 +191,7 @@
     da_ref[...] = jnp.zeros_like(da_ref)
     db_ref[...] = jnp.zeros_like(db_ref)
 
-    @pl.loop(0, count)
-    def _(j):
-        pltpu.make_async_copy(
-            slots[0].at[:, 2 * width : 3 * width], held.at[j], sem_q.at[j]
-        ).wait()
-        pltpu.make_async_copy(own[0], left.at[j], sem_l.at[j]).wait()
-        pltpu.make_async_copy(other[0], right.at[j], sem_r.at[j]).wait()
+    def body(j):
         queries = held[j]
         d_out = halves(left[j] + right[j])
         a = (ah[...], al[...])
@@ -191,7 +212,11 @@
         )
         dq_held[j] = back.astype(bf16)
 
-    copies = [pltpu.make_async_copy(dq_held.at[j], dq[j], sem_o.at[j]) for j in range(count)]
+    rows = slots[0].shape[0]
+    joined_loop(count, rows, waits, body)
+    copies = [
+        pltpu.make_async_copy(dq_held.at[part(j, rows)], dq[j], sem_o.at[j]) for j in range(count)
+    ]
     for copy in copies:
         copy.start()
     total = jnp.sum(ga_ref[...] * da_ref[...]) + jnp.sum(gb_ref[...] * db_ref[...])
@@ -210,14 +235,14 @@
         in_specs=[any_spec()] * (3 * count) + [vmem_spec()] * (len(sums) + 4),
         out_specs=[vmem_spec()] * 3 + [any_spec()] * count,
         scratch_shapes=[
-            pltpu.VMEM((count, rows, width), bf16),
-            pltpu.VMEM((count, rows, width), f32),
-            pltpu.VMEM((count, rows, width), f32),
+            pltpu.VMEM((count * rows, width), bf16),
+            pltpu.VMEM((count * rows, width), f32),
+            pltpu.VMEM((count * rows, width), f32),
             pltpu.VMEM((width, 2 * width), bf16),
             pltpu.VMEM((width, 2 * width), bf16),
             pltpu.VMEM((width, width), bf16),
             pltpu.VMEM((width, width), bf16),
-            pltpu.VMEM((count, rows, width), bf16),
+            pltpu.VMEM((count * rows, width), bf16),
             pltpu.SemaphoreType.DMA((count,)),
             pltpu.SemaphoreType.DMA((count,)),
             pltpu.SemaphoreType.DMA((count,)),
@@ -241,10 +266,12 @@
     held, dah, dal, dbh, dbl, out_held, sem_k, sem_o = refs[:8]
     kept_held, kept_sems = refs[8 : 8 + n_kept], refs[8 + n_kept :]
     width = wb_ref.shape[0]
-    fetch_all(slots, held, sem_k)
+    rows = slots[0].shape[0]
+    waits = [fetch(slots, held, sem_k)]
     for source, target, sems in zip(kept, kept_held, kept_sems):
-        for j in range(count):
-            pltpu.make_async_copy(source.at[first + j], target.at[j], sems.at[j]).start()
+        waits.append(
+            fetch([source.at[part(first + j, rows)] for j in range(count)], target, sems)
+        )
     gain = gain_ref[0]
     rms, scale = scale_of(sums, entries)
     product = dots[0][0:1, 0:1]
@@ -259,12 +286,8 @@
             (d_ref[...] * (1.0 / scale) - g_ref[...] * pull) * (-inner_rate)
         )
 
-    @pl.loop(0, count)
-    def _(j):
-        pltpu.make_async_copy(slots[0], held.at[j], sem_k.at[j]).wait()
-        for source, target, sems in zip(kept, kept_held, kept_sems):
-            pltpu.make_async_copy(source.at[first], target.at[j], sems.at[j]).wait()
-        keys = held[j, :, :width]
+    def body(j):
+        keys = held[j, :width]
         mixed = nn(keys, wa_ref[...]) * gain
         moved = two_right(nn, keys, (dah[...], dal[...])) * gain
         u, w = mixed[:, :width], mixed[:, width:]
@@ -277,11 +300,11 @@
         db = (dbh[...], dbl[...])
         hidden = halves(act * w)
         shift = two(nn, halves(slope * du * w + act * dw), wb_ref[...]) + three(nn, hidden, db)
-        out_held[j, :, width:] = (-shift).astype(bf16)
+        out_held[j, width:] = (-shift).astype(bf16)
         if n_kept:
             e2, hb = halves(kept_held[0][j]), kept_held[1][j]
         else:
-            values = held[j, :, width : 2 * width].astype(f32)
+            values = held[j, width : 2 * width].astype(f32)
             e2 = halves(two(nn, hidden, wb_ref[...]) - values)
             hb = two(nt, e2, wb_ref[...])
         back = two(nt, halves(shift), wb_ref[...]) + three(nt, e2, db)
@@ -295,9 +318,12 @@
             + three(nt, ut, (dah[:, :width], dal[:, :width]))
             + three(nt, wt, (dah[:, width:], dal[:, width:]))
         )
-        out_held[j, :, :width] = (grad * gain).astype(bf16)
-
-    copies = [pltpu.make_async_copy(out_held.at[j], out[j], sem_o.at[j]) for j in range(count)]
+        out_held[j, :width] = (grad * gain).astype(bf16)
+
+    joined_loop(count, rows, waits, body)
+    copies = [
+        pltpu.make_async_copy(out_held.at[part(j, rows)], out[j], sem_o.at[j]) for j in range(count)
+    ]
     for copy in copies:
         copy.start()
     for copy in copies:
@@ -317,16 +343,16 @@
         + [any_spec()] * len(kept),
         out_specs=[any_spec()] * count,
         scratch_shapes=[
-            pltpu.VMEM((count,) + slots[0].shape, bf16),
+            pltpu.VMEM((count * rows, slots[0].shape[1]), bf16),
             pltpu.VMEM((width, 2 * width), bf16),
             pltpu.VMEM((width, 2 * width), bf16),
             pltpu.VMEM((width, width), bf16),
             pltpu.VMEM((width, width), bf16),
-            pltpu.VMEM((count, rows, 2 * width), bf16),
+            pltpu.VMEM((count * rows, 2 * width), bf16),
             pltpu.SemaphoreType.DMA((count,)),
             pltpu.SemaphoreType.DMA((count,)),
         ]
-        + [pltpu.VMEM((count, rows, width), f32)] * len(kept)
+        + [pltpu.VMEM((count * rows, width), f32)] * len(kept)
         + [pltpu.SemaphoreType.DMA((count,))] * len(kept),
         compiler_params=pltpu.CompilerParams(vmem_limit_bytes=vmem_bytes),
         cost_estimate=estimate(26, rows * count),
@@ -334,7 +360,7 @@
     )(*slots, *sums, *dots, gain, wa, wb, ga, gb, da, db, *kept)
 
 
-def per_device(queries, keys, values, fast_in, fast_out, key_gain, out_proj, grad_out):
+def any_line(queries, keys, values, fast_in, fast_out, key_gain, out_proj, grad_out):
     toks, heads = lax.axis_size("tok"), lax.axis_size("head")
     low, high = toks // 2 - 1, toks // 2
     width = fast_out.shape[1]
@@ -366,20 +392,13 @@
     ga, gb, squares, *kept = call_inner_grad(slots, toks <= 8, key_gain, wa, wb)
 
     def exchange(value):
-        across = [
-            (flat(root(h), h), flat(root(h ^ 1), h ^ 1)) for h in range(heads)
-        ]
-        value = value + lax.ppermute(value, both, across)
-        step = 2
-        while step < heads:
-            far = [(flat(root(h), h), flat(root(h), h ^ step)) for h in range(heads)]
-            more = lax.ppermute(value, both, far)
-            step *= 2
-            if step < heads:
-                value = value + more
-            else:
-                return value, more
-        return (value,)
+        parts = [value]
+        for step in range(1, heads):
+            turn = [(h, (h + step) % heads) for h in range(heads)]
+            parts.append(
+                lax.ppermute(value, both, [(flat(root(a), a), flat(root(b), b)) for a, b in turn])
+            )
+        return parts
 
     sums = exchange(squares)
 
@@ -449,6 +468,422 @@
     )
     pair = home(list(outs_near) + list(outs_far))
     return d_queries, pair[:, :width], pair[:, width:]
+
+
+def call(kernel, name, units, rows, out_shape, out_specs, operands, scratch):
+    light = name == "gradient"
+    return pl.pallas_call(
+        kernel,
+        out_shape=out_shape,
+        in_specs=[spec for _, spec in operands],
+        out_specs=out_specs,
+        scratch_shapes=scratch,
+        compiler_params=pltpu.CompilerParams(vmem_limit_bytes=vmem_bytes),
+        cost_estimate=estimate(0.01 if light else units, rows),
+        name=name,
+    )(*(value for value, _ in operands))
+
+
+def held_rows(count, rows, columns, dtype):
+    return [pltpu.VMEM((count * rows, columns), dtype), pltpu.SemaphoreType.DMA((count,))]
+
+
+def gradient_kernel(count, *refs):
+    slots = refs[:count]
+    gain_ref, wa_ref, wb_ref, g_ref, sq_ref, kept, held, sems, misfit, sem_m = refs[count:]
+    wait = fetch(slots, held, sems)
+    gain = gain_ref[0]
+    width, rows = wb_ref.shape[0], slots[0].shape[0]
+    g_ref[...] = jnp.zeros_like(g_ref)
+
+    @pl.loop(0, count)
+    def _(j):
+        wait(j)
+        here = part(j, rows)
+        keys = held[here, :width]
+        values = held[here, width : 2 * width].astype(f32)
+        mixed = nn(keys, wa_ref[...]) * gain
+        u, w = mixed[:, :width], mixed[:, width:]
+        sg = sigmoid(u)
+        act = u * sg
+        hidden = halves(act * w)
+        e = two(nn, hidden, wb_ref[...]) - values
+        misfit[here, :width] = e
+        e2 = halves(e)
+        hb = two(nt, e2, wb_ref[...])
+        misfit[here, width:] = hb
+        pltpu.make_async_copy(misfit.at[here], kept.at[here], sem_m.at[j]).start()
+        g_ref[:, 2 * width :] += three(tn, hidden, e2)
+        slope = sg * (1.0 + u * (1.0 - sg))
+        g_ref[:, :width] += two_right(tn, keys, halves(hb * w * slope))
+        g_ref[:, width : 2 * width] += two_right(tn, keys, halves(hb * act))
+
+    ga = g_ref[:, : 2 * width] * gain
+    g_ref[:, : 2 * width] = ga
+    gb = g_ref[:, 2 * width :]
+    sq_ref[...] = jnp.zeros_like(sq_ref) + (jnp.sum(ga * ga) + jnp.sum(gb * gb))
+    for j in range(count):
+        here = part(j, rows)
+        pltpu.make_async_copy(misfit.at[here], kept.at[here], sem_m.at[j]).wait()
+
+
+def call_gradient(slots, gain, wa, wb):
+    count, (rows, columns) = len(slots), slots[0].shape
+    width = wb.shape[0]
+    return call(
+        partial(gradient_kernel, count),
+        "gradient",
+        13,
+        rows * count,
+        (shape_of(width, 3 * width), shape_of(8, 128), shape_of(count * rows, 2 * width)),
+        [vmem_spec(), vmem_spec(), any_spec()],
+        [(x, any_spec()) for x in slots]
+        + [(gain, smem_spec()), (wa, vmem_spec()), (wb, vmem_spec())],
+        held_rows(count, rows, columns, bf16) + held_rows(count, rows, 2 * width, f32),
+    )
+
+
+def pull_query_kernel(opening, entries, *refs):
+    slots, own, other = refs[:2], refs[2:4], refs[4:6]
+    if opening:
+        g_all, sum0, sum1, wa_ref, wb_ref, acc_ref, uh, ul, dq0, dq1 = refs[6:16]
+    else:
+        g_all, old, uh, ul, acc_ref, p_ref, mh, ml = refs[6:14]
+    held, sem_q, left, sem_l, right, sem_r, g_ref, sem_g, sem_a = refs[-9:]
+    width, rows = held.shape[1], slots[0].shape[0]
+    both_in, gate, up, down = (
+        slice(0, 2 * width),
+        slice(0, width),
+        slice(width, 2 * width),
+        slice(2 * width, 3 * width),
+    )
+    waits = [
+        fetch([block.at[:, down] for block in slots], held, sem_q),
+        fetch(own, left, sem_l),
+        fetch(other, right, sem_r),
+    ]
+    g_wait = fetch([g_all], g_ref, sem_g)
+    if opening:
+        g_wait(0)
+        _, scale = scale_of((sum0, sum1), entries)
+        rate = inner_rate / scale
+        for w_ref, place in ((wa_ref, both_in), (wb_ref, down)):
+            uh[:, place], ul[:, place] = halves(w_ref[...].astype(f32) - g_ref[:, place] * rate)
+        acc_ref[...] = jnp.zeros_like(acc_ref)
+    else:
+        a_wait = fetch([old], acc_ref, sem_a)
+
+    @pl.loop(0, 2)
+    def _(j):
+        for wait in waits:
+            wait(j)
+        here = part(j, rows)
+        queries = held[here]
+        d_out = halves(left[here] + right[here])
+        mixed = two_right(nn, queries, (uh[:, both_in], ul[:, both_in]))
+        u, w = mixed[:, :width], mixed[:, width:]
+        sg = sigmoid(u)
+        act = u * sg
+        hb = three(nt, d_out, (uh[:, down], ul[:, down]))
+        if not opening:
+
+            @pl.when(j == 0)
+            def _():
+                a_wait(0)
+
+        acc_ref[:, down] += three(tn, halves(act * w), d_out)
+        slope = sg * (1.0 + u * (1.0 - sg))
+        ub = halves(hb * w * slope)
+        wbar = halves(hb * act)
+        acc_ref[:, gate] += two_right(tn, queries, ub)
+        acc_ref[:, up] += two_right(tn, queries, wbar)
+        if not opening:
+            for m_ref, gate_part, up_part in ((mh, ub[0], wbar[0]), (ml, ub[1], wbar[1])):
+                m_ref[here, :width] = gate_part
+                m_ref[here, width:] = up_part
+            return
+        back = three(nt, ub, (uh[:, gate], ul[:, gate])) + three(
+            nt, wbar, (uh[:, up], ul[:, up])
+        )
+        for k, dq_ref in enumerate((dq0, dq1)):
+
+            @pl.when(j == k)
+            def _():
+                dq_ref[...] = back.astype(bf16)
+
+    if not opening:
+        g_wait(0)
+        p_ref[...] = jnp.zeros_like(p_ref) + jnp.sum(g_ref[...] * acc_ref[...])
+
+
+def query_grad_kernel(mh, ml, uh, ul, *dqs):
+    width = uh.shape[0]
+    rows = mh.shape[0] // 2
+    both_in = slice(0, 2 * width)
+    for k, dq_ref in enumerate(dqs):
+        here = slice(k * rows, (k + 1) * rows)
+        back = three(nt, (mh[here], ml[here]), (uh[:, both_in], ul[:, both_in]))
+        dq_ref[...] = back.astype(bf16)
+
+
+def call_query_grad(mh, ml, uh, ul):
+    rows, width = mh.shape[0] // 2, uh.shape[0]
+    return call(
+        query_grad_kernel,
+        "query_grad",
+        6,
+        2 * rows,
+        (shape_of(rows, width, dtype=bf16),) * 2,
+        [vmem_spec()] * 2,
+        [(x, vmem_spec()) for x in (mh, ml, uh, ul)],
+        [],
+    )
+
+
+def call_pull_query(entries, slots, own, other, streams, more, opening):
+    rows, width = slots[0].shape[0], slots[0].shape[1] // 3
+    whole = shape_of(width, 3 * width)
+    half = shape_of(width, 3 * width, dtype=bf16)
+    dq = shape_of(rows, width, dtype=bf16)
+    mixed = shape_of(2 * rows, 2 * width, dtype=bf16)
+    outs = (whole, half, half, dq, dq) if opening else (whole, shape_of(8, 128), mixed, mixed)
+    return call(
+        partial(pull_query_kernel, opening, entries),
+        "query_pull",
+        20,
+        rows * 2,
+        outs,
+        [vmem_spec()] * len(outs),
+        [(x, any_spec()) for x in (*slots, *own, *other, *streams)]
+        + [(x, vmem_spec()) for x in more],
+        held_rows(2, rows, width, bf16)
+        + held_rows(2, rows, width, f32)
+        + held_rows(2, rows, width, f32)
+        + held_rows(1, width, 3 * width, f32)
+        + [pltpu.SemaphoreType.DMA((1,))],
+    )
+
+
+def pull_key_kernel(entries, blocks, *refs):
+    count = len(blocks)
+    slots, refs = refs[:count], refs[count:]
+    kept, gain_ref, wa_ref, wb_ref = refs[:4]
+    sum0, sum1, dot0, dot1, g_ref, du_ref = refs[4:10]
+    out, scratch = refs[10 : 10 + count], refs[10 + count :]
+    held, sem_k, kept_held, sem_e, dh, dl = scratch
+    width, rows = wb_ref.shape[0], slots[0].shape[0]
+    waits = [
+        fetch(slots, held, sem_k),
+        fetch([kept.at[part(block, rows)] for block in blocks], kept_held, sem_e),
+    ]
+    gain = gain_ref[0]
+    rms, scale = scale_of((sum0, sum1), entries)
+    pull = (dot0[0:1, 0:1] + dot1[0:1, 0:1]) / (scale * scale * entries * rms)
+    dh[...], dl[...] = halves((du_ref[...] * (1.0 / scale) - g_ref[...] * pull) * (-inner_rate))
+    both_in, gate, up, down = (
+        slice(0, 2 * width),
+        slice(0, width),
+        slice(width, 2 * width),
+        slice(2 * width, 3 * width),
+    )
+
+    @pl.loop(0, count)
+    def _(j):
+        for wait in waits:
+            wait(j)
+        here = part(j, rows)
+        keys = held[here, :width]
+        mixed = nn(keys, wa_ref[...]) * gain
+        moved = two_right(nn, keys, (dh[:, both_in], dl[:, both_in])) * gain
+        u, w = mixed[:, :width], mixed[:, width:]
+        du, dw = moved[:, :width], moved[:, width:]
+        sg = sigmoid(u)
+        act = u * sg
+        rest = 1.0 - sg
+        slope = sg * (1.0 + u * rest)
+        bend = sg * rest * (2.0 + u * (rest - sg))
+        db = (dh[:, down], dl[:, down])
+        shift = two(nn, halves(slope * du * w + act * dw), wb_ref[...]) + three(
+            nn, halves(act * w), db
+        )
+        back = two(nt, halves(shift), wb_ref[...]) + three(
+            nt, halves(kept_held[here, :width]), db
+        )
+        hb = kept_held[here, width:]
+        ub = halves(back * w * slope + hb * (bend * du * w + slope * dw))
+        wbar = halves(back * act + hb * slope * du)
+        ut = halves(hb * slope * w)
+        wt = halves(hb * act)
+        grad = (
+            two(nt, ub, wa_ref[:, :width])
+            + two(nt, wbar, wa_ref[:, width:])
+            + three(nt, ut, (dh[:, gate], dl[:, gate]))
+            + three(nt, wt, (dh[:, up], dl[:, up]))
+        )
+        for k, out_ref in enumerate(out):
+
+            @pl.when(j == k)
+            def _():
+                out_ref[:, :width] = (grad * gain).astype(bf16)
+                out_ref[:, width:] = (-shift).astype(bf16)
+
+
+def call_pull_key(blocks, entries, slots, kept, gain, wa, wb, terms):
+    count, (rows, columns) = len(blocks), slots[0].shape
+    width = wb.shape[0]
+    return call(
+        partial(pull_key_kernel, entries, blocks),
+        "key_pull",
+        26,
+        rows * count,
+        (shape_of(rows, 2 * width, dtype=bf16),) * count,
+        [vmem_spec()] * count,
+        [(slots[block], any_spec()) for block in blocks]
+        + [(kept, any_spec()), (gain, smem_spec()), (wa, vmem_spec()), (wb, vmem_spec())]
+        + [(x, vmem_spec()) for x in terms],
+        held_rows(count, rows, columns, bf16)
+        + held_rows(count, rows, 2 * width, f32)
+        + [pltpu.VMEM((width, 3 * width), bf16)] * 2,
+    )
+
+
+def four_line(queries, keys, values, fast_in, fast_out, key_gain, out_proj, grad_out):
+    toks, heads = 4, lax.axis_size("head")
+    low, high = 1, 2
+    width = fast_out.shape[1]
+    entries = float(heads * (fast_in.shape[1] * fast_in.shape[2] + width * fast_out.shape[2]))
+    place, head = lax.axis_index("tok"), lax.axis_index("head")
+    core = lax.rem(head, 2)
+    line, mirror = (1, 0, 2, 3), (2, 3, 1, 0)
+    both = ("tok", "head")
+    tie = lax.optimization_barrier
+
+    def flat(t, h):
+        return t * heads + h
+
+    def root(h):
+        return high if h % 2 else low
+
+    def order(h):
+        return mirror if h % 2 else line
+
+    def to_root(j):
+        return [(flat(order(h)[j], h), flat(root(h), h)) for h in range(heads)]
+
+    def home(value, j):
+        return lax.ppermute(value, both, [(b, a) for a, b in to_root(j)])
+
+    is_root = place == jnp.where(core == 0, low, high)
+    wa, wb = fast_in[0], fast_out[0]
+    rows_in = jnp.concatenate([keys, values, queries], axis=1)
+    slots = [rows_in] + [lax.ppermute(rows_in, both, to_root(j)) for j in range(1, toks)]
+
+    far = lax.ppermute(out_proj, "tok", [(0, low), (3, high)])
+    quarter = grad_out.shape[1] // 4
+
+    def columns(array, which, half_is_low):
+        index = jnp.where(half_is_low, 1 - which, 2 + which)
+        return lax.dynamic_slice_in_dim(array, index * quarter, quarter, axis=1)
+
+    def piece(array, j):
+        return lax.ppermute(
+            columns(array, core, place == line[j]), "tok", [(line[j], low), (mirror[j], high)]
+        )
+
+    def swap_cores(value):
+        return lax.ppermute(value, "head", [(h, h ^ 1) for h in range(heads)])
+
+    piece2 = piece(grad_out, 2)
+    later, far, piece2, *slots = tie((grad_out, far, piece2, *slots))
+
+    def exchange(value, pairs, step_pairs, beside=None):
+        more = lax.ppermute(value, both, pairs)
+        if beside is not None:
+            outs, more = tie((beside(), more))
+        value = value + more
+        step = 2
+        while True:
+            more = lax.ppermute(value, both, step_pairs(step))
+            step *= 2
+            if step >= heads:
+                return (value, more) if beside is None else (value, more, outs)
+            value = value + more
+
+    over = [
+        (flat(high, h), flat(low, h)) if h % 2 == 0 else (flat(low, h), flat(high, h))
+        for h in range(heads)
+    ]
+    root_pairs = [(flat(root(h), h), flat(root(h ^ 1), h ^ 1)) for h in range(heads)]
+
+    def root_steps(step):
+        return [(flat(root(h), h), flat(root(h), h ^ step)) for h in range(heads)]
+
+    at_low = place <= low
+    piece3 = piece(later, 3)
+    piece1 = piece(later, 1)
+    g, squares, kept = call_gradient(slots, key_gain, wa, wb)
+    g, squares, far, piece2, mine0, theirs0 = tie(
+        (
+            g,
+            squares,
+            far,
+            piece2,
+            columns(later, core, at_low),
+            columns(later, 1 - core, at_low),
+        )
+    )
+
+    w_mine = jnp.where(core == 0, out_proj, far)
+    w_theirs = jnp.where(core == 0, far, out_proj)
+
+    def product(mine, theirs):
+        return nt(mine, w_mine) + nt(theirs, w_theirs)
+
+    own0 = product(mine0, theirs0)
+    other2 = lax.ppermute(own0, both, over)
+    own2 = product(piece2, swap_cores(piece2))
+    other0 = lax.ppermute(own2, both, over)
+    squares_in, *_ = tie((squares, own0, own2))
+    sums = exchange(squares_in, root_pairs, root_steps)
+    piece3, piece1, other0, other2, *sums = tie((piece3, piece1, other0, other2, *sums))
+
+    own3 = product(piece3, swap_cores(piece3))
+    other1 = lax.ppermute(own3, both, over)
+    own1 = product(piece1, swap_cores(piece1))
+    other3 = lax.ppermute(own1, both, over)
+    own3, own1, *sums = tie((own3, own1, *sums))
+    acc, uh, ul, dq0, dq2 = call_pull_query(
+        entries, slots[0::2], (own0, own2), (other0, other2), (g,), (*sums, wa, wb), True
+    )
+    other1, other3, acc, uh, ul, dq2 = tie((other1, other3, acc, uh, ul, dq2))
+
+    du, dots, mh, ml = call_pull_query(
+        entries, slots[1::2], (own1, own3), (other1, other3), (g, acc), (uh, ul), False
+    )
+    du, dots, mh, ml = tie((du, dots, mh, ml))
+
+    *dots, (dq1, dq3) = exchange(
+        dots, root_pairs, root_steps, lambda: call_query_grad(mh, ml, uh, ul)
+    )
+    du, dq1, dq3, *dots = tie((du, dq1, dq3, *dots))
+
+    terms = (*sums, *dots, g, du)
+    dq1, dq2, dq3 = home(dq1, 1), home(dq2, 2), home(dq3, 3)
+    out3, out2 = call_pull_key((3, 2), entries, slots, kept, key_gain, wa, wb, terms)
+    out3, out2, dq1, dq2, dq3, *terms = tie((out3, out2, dq1, dq2, dq3, *terms))
+
+    out3, out2 = home(out3, 3), home(out2, 2)
+    out1, out0 = call_pull_key((1, 0), entries, slots, kept, key_gain, wa, wb, terms)
+    d_queries = jnp.where(is_root, dq0, dq1 + dq2 + dq3)
+    out3, out2, out1, out0, d_queries = tie((out3, out2, out1, out0, d_queries))
+
+    pair = jnp.where(is_root, out0, home(out1, 1) + out2 + out3)
+    return d_queries, pair[:, :width], pair[:, width:]
+
+
+def per_device(*arrays):
+    fits = lax.axis_size("tok") == 4 and lax.axis_size("head") >= 4
+    return (four_line if fits else any_line)(*arrays)
 
 
 def solution(mesh):

time: 179 us -> 177 us (0.989)
  Pallas kernels: 60.8 us -> 73.4 us
  waiting for transfers between devices: 62.8 us -> 55.3 us
  starting transfers between devices: 35.3 us -> 31.8 us
  local copies, waits for them, and re-layouts: 8.81 us -> 6.08 us
    pallas_call x4 -> x6, Pallas kernels: 60.8 us -> 73.4 us  [call(): pl.pallas_call(kernel, out_shape=out_shape, in_specs=[spec for _, spec in...]
    ppermute x24, waiting for transfers between devices: 62.8 us -> 55.3 us  [the longest x3 27 us: four_line(): lax.ppermute(rows_in, both, to_root(j))]
    ppermute x24, starting transfers between devices: 35.3 us -> 31.8 us  [the longest x3 8.4 us: piece(): lax.ppermute(columns(array, core, place == line[j]), 'tok', [(line[j], lo...]
    unnamed x44 -> x40, local copies, waits for them, and re-layouts: 4.86 us -> 2.98 us
  transfers between devices with their start and end apart: 24 -> 24, of which waited for: 3 -> 4; matrix products, arithmetic and copies ran while one was open for 7% -> 6% of each run, Pallas kernels for 23% -> 35%
where the time goes in v2:
time: 177 us; the launch traced here: 176 us
  Pallas kernels  73.4 us (41%)
  waiting for transfers between devices  55.3 us (31%)
  starting transfers between devices  31.8 us (18%)
  local copies, waits for them, and re-layouts  6.08 us (3%)
  matrix products  4.87 us (3%)
  other arithmetic  2.24 us (1%)
  between operations  1.98 us (1%)
    pallas_call x6, Pallas kernels, call(): pl.pallas_call(kernel, out_shape=out_shape, in_specs=[spec for _, spec in...  73.4 us
    ppermute x3, waiting for transfers between devices, four_line(): lax.ppermute(rows_in, both, to_root(j))  27 us
    ppermute x6, waiting for transfers between devices, home(): return lax.ppermute(value, both, [(b, a) for a, b in to_root(j)])  26.8 us
    ppermute x3, starting transfers between devices, piece(): lax.ppermute(columns(array, core, place == line[j]), 'tok', [(line[j], lo...  8.4 us
    ppermute x1, starting transfers between devices, four_line(): far = lax.ppermute(out_proj, 'tok', [(0, low), (3, high)])  6.09 us
    ppermute x6, starting transfers between devices, home(): return lax.ppermute(value, both, [(b, a) for a, b in to_root(j)])  5.54 us
    ppermute x3, starting transfers between devices, four_line(): lax.ppermute(rows_in, both, to_root(j))  5.31 us
    dot_general x8, matrix products, nt(): lax.dot_general(a, b, (((1,), (1,)), ((), ())), preferred_element_type=f32)  4.87 us
  transfers between devices with their start and end apart: 24, of which 4 were waited for; matrix products, arithmetic and copies ran while one was open for 6% of the time, Pallas kernels for 35%

profile of v2, /device:TPU:0, one launch (start us, length us, event | category | flops | bytes accessed | tf_op | source)
XLA Modules:
  0.0 175.6 jit_solution(18050718319693887627)
XLA Ops:
  0.6 0.0 copy-start
  0.6 6.1 %collective-permute-start = (bf16[512,1024]{1,0:T(8,128)(2,1)}, bf16[512,1024]{1,0:T(8,128)(2,1)}, u32[]{:S(2)}, u32[]{:S(2)}) collective-permute-start(bf16[512,1024]{1,0:T(8,128)(2,1)} %param.14), channel_id=1, source_target_pairs={{0,4},{12,8},{1,5},{13,9},{2,6},{14,10},{3,7},{15,11},{16,20},{28,... | collective-permute-start | bytes 3145736 | tf_op jit(solution)/shard_map/ppermute | solution.py:781
  6.7 1.0 constant_dynamic-update-slice_fusion.2
  7.7 1.0 constant_dynamic-update-slice_fusion.1
  8.7 1.0 constant_dynamic-update-slice_fusion.refs_0_.refs_1_
  9.7 1.6 collective-permute-start.4
  11.3 1.6 collective-permute-start.3
  12.8 2.2 %collective-permute-start.2 = (bf16[256,1536]{1,0:T(8,128)(2,1)S(1)}, bf16[256,1536]{1,0:T(8,128)(2,1)}, u32[]{:S(2)}, u32[]{:S(2)}) collective-permute-start(bf16[256,1536]{1,0:T(8,128)(2,1)S(1)} %constant_dynamic-update-slice_fusion.refs_0_.refs_1_), channel_id=1, source_target_pairs={{0,4},{13,9},{2,6},{15,11},{16,20},{29,25},{18,22},{31,27}} | collective-permute-start | bytes 2359304 | tf_op jit(solution)/shard_map/ppermute | solution.py:779
  15.0 1.1 constant_dynamic-slice_fusion.4
  16.1 1.5 collective-permute-start.1
  18.2 0.0 collective-permute-done.4.refs_3_.refs_1_.refs_0_
  18.2 26.9 %collective-permute-done.2.refs_1_.refs_0_ = bf16[256,1536]{1,0:T(8,128)(2,1)} collective-permute-done((bf16[256,1536]{1,0:T(8,128)(2,1)S(1)}, bf16[256,1536]{1,0:T(8,128)(2,1)}, u32[]{:S(2)}, u32[]{:S(2)}) %collective-permute-start.2) | collective-permute-done | bytes 786464 | tf_op jit(solution)/shard_map/ppermute | solution.py:779
  45.2 0.0 collective-permute-done
  45.2 0.2 constant_dynamic-slice_fusion
  45.4 5.6 %collective-permute-start.6 = (bf16[256,1024]{1,0:T(8,128)(2,1)S(1)}, bf16[256,1024]{1,0:T(8,128)(2,1)S(1)}, u32[]{:S(2)}, u32[]{:S(2)}) collective-permute-start(bf16[256,1024]{1,0:T(8,128)(2,1)S(1)} %get-tuple-element.151), channel_id=1, source_target_pairs={{0,4},{12,8},{1,5},{13,9},{2,6},{14,10},{3,7},{15,11},{16,20},{28,... | collective-permute-start | bytes 1572872 | tf_op jit(solution)/shard_map/ppermute | solution.py:789
  51.0 1.3 collective-permute-start.5
  52.4 0.0 copy-start.2
  52.4 14.0 %gradient.1 = (f32[512,1536]{1,0:T(8,128)}, f32[8,128]{1,0:T(8,128)}, f32[1024,1024]{1,0:T(8,128)}) custom-call(bf16[256,1536]{1,0:T(8,128)(2,1)} %copy-done.1, bf16[256,1536]{1,0:T(8,128)(2,1)} %collective-permute-done.2.refs_1_.refs_0_, bf16[256,1536]{1,0:T(8,128)(2,1)} %collective-permute-done.3.refs_2_.refs_1_, ...), custom_call_target="tpu_custom_call" | custom-call | flops 5368709 | bytes 1048576 | tf_op jit(solution)/shard_map/gradient/pallas_call | solution.py:475
  66.4 0.1 collective-permute-start.7
  66.5 1.4 broadcast_select_fusion
  67.9 0.5 fusion.2
  68.3 0.5 convolution_add_fusion.2.refs_2_
  68.8 0.0 copy-start.10
  68.9 0.8 collective-permute-start.9
  69.7 1.5 fusion.1
  71.2 0.5 convolution_add_fusion.3.refs_3_
  71.7 0.7 collective-permute-start.8
  72.4 0.7 collective-permute-start.10
  73.1 0.0 collective-permute-done.10
  73.2 0.7 collective-permute-start.11
  73.8 0.0 collective-permute-done.6
  73.8 0.0 collective-permute-done.9.refs_5_
  73.9 0.6 collective-permute-start.12
  74.5 0.1 collective-permute-start.13
  74.5 1.5 collective-permute-done.12
  76.0 0.5 fusion.3
  76.5 0.5 convolution_add_fusion.1.refs_3_
  77.0 0.7 collective-permute-start.14
  77.7 0.5 fusion.4
  78.2 0.5 convolution_add_fusion.refs_2_
  78.7 0.9 collective-permute-start.15
  79.6 14.7 %query_pull.2 = (f32[512,1536]{1,0:T(8,128)}, bf16[512,1536]{1,0:T(8,128)(2,1)}, bf16[512,1536]{1,0:T(8,128)(2,1)}, bf16[256,512]{1,0:T(8,128)(2,1)}, bf16[256,512]{1,0:T(8,128)(2,1)}) custom-call(bf16[256,1536]{1,0:T(8,128)(2,1)} %copy-done.1, bf16[256,1536]{1,0:T(8,128)(2,1)} %collective-permute-done.3.refs_2_.refs_1_, f32[256,512]{1,0:T(8,128)} %copy-done.3, ...), custom_call_target="tpu_custom_call" | custom-call | flops 5368709120 | bytes 1048576 | tf_op jit(solution)/shard_map/query_pull/pallas_call | solution.py:475
  94.3 0.8 copy-done.14
  95.1 0.2 copy-done.15
  95.3 11.4 %query_pull.3 = (f32[512,1536]{1,0:T(8,128)}, f32[8,128]{1,0:T(8,128)}, bf16[512,1024]{1,0:T(8,128)(2,1)}, bf16[512,1024]{1,0:T(8,128)(2,1)}) custom-call(bf16[256,1536]{1,0:T(8,128)(2,1)} %collective-permute-done.2.refs_1_.refs_0_, bf16[256,1536]{1,0:T(8,128)(2,1)} %collective-permute-done.4.refs_3_.refs_1_.refs_0_, f32[256,512]{1,0:T(8,128)} %copy-done.6, ...), custom_call_target="tpu_custom_call" | custom-call | flops 5368709120 | bytes 1048576 | tf_op jit(solution)/shard_map/query_pull/pallas_call | solution.py:475
  106.7 0.7 collective-permute-start.16
  107.3 0.0 copy-start.16
  107.3 5.1 %query_grad.1 = (bf16[256,512]{1,0:T(8,128)(2,1)}, bf16[256,512]{1,0:T(8,128)(2,1)}) custom-call(bf16[512,1024]{1,0:T(8,128)(2,1)} %get-tuple-element.112.mh, bf16[512,1024]{1,0:T(8,128)(2,1)} %get-tuple-element.113.ml, bf16[512,1536]{1,0:T(8,128)(2,1)} %get-tuple-element.109.refs_8_.uh, bf16[512,1536]{1,0:T(8,128)(2,1)} %get-tuple-element.110.refs_9_.ul), custom_call_target="tpu_custom_call" | custom-call | flops 1610612736 | bytes 1048576 | tf_op jit(solution)/shard_map/query_grad/pallas_call | solution.py:475
  112.4 0.7 collective-permute-start.17
  113.1 0.7 collective-permute-start.19
  113.8 0.0 copy-start.18
  113.8 1.3 collective-permute-start.18
  115.1 0.9 collective-permute-start.20
  116.1 0.0 copy-start.7
  116.1 14.1 %key_pull.2 = (bf16[256,1024]{1,0:T(8,128)(2,1)}, bf16[256,1024]{1,0:T(8,128)(2,1)}) custom-call(bf16[256,1536]{1,0:T(8,128)(2,1)} %collective-permute-done.4.refs_3_.refs_1_.refs_0_, bf16[256,1536]{1,0:T(8,128)(2,1)} %collective-permute-done.3.refs_2_.refs_1_, f32[1024,1024]{1,0:T(8,128)} %get-tuple-element.79.refs_2_, f32[1]{0:T(128)S(6)} %copy.13.refs_4_.refs_3_, ...), custom_call_target="tpu_custom_call" | custom-call | flops 6979321856 | bytes 1048576 | tf_op jit(solution)/shard_map/key_pull/pallas_call | solution.py:475
  130.2 9.8 %collective-permute-done.18 = bf16[256,512]{1,0:T(8,128)(2,1)S(1)} collective-permute-done((bf16[256,512]{1,0:T(8,128)(2,1)}, bf16[256,512]{1,0:T(8,128)(2,1)S(1)}, u32[]{:S(2)}, u32[]{:S(2)}) %collective-permute-start.18) | collective-permute-done | bytes 262176 | tf_op jit(solution)/shard_map/ppermute | solution.py:774
  140.0 0.7 collective-permute-start.21
  140.7 0.7 collective-permute-start.22
  141.4 0.8 add_select_fusion.1
  142.2 14.2 %key_pull.3 = (bf16[256,1024]{1,0:T(8,128)(2,1)}, bf16[256,1024]{1,0:T(8,128)(2,1)}) custom-call(bf16[256,1536]{1,0:T(8,128)(2,1)} %collective-permute-done.2.refs_1_.refs_0_, bf16[256,1536]{1,0:T(8,128)(2,1)} %copy-done.1, f32[1024,1024]{1,0:T(8,128)} %get-tuple-element.79.refs_2_, f32[1]{0:T(128)S(6)} %copy.13.refs_4_.refs_3_, bf16[512,1024]{1,0:T(8,128)(2,1)} %bitcast.21, ...), custom_call_target="tpu_custom_call" | custom-call | flops 6979321856 | bytes 1048576 | tf_op jit(solution)/shard_map/key_pull/pallas_call | solution.py:475
  156.4 1.3 collective-permute-start.23
  157.7 17.0 %collective-permute-done.23 = bf16[256,1024]{1,0:T(8,128)(2,1)S(1)} collective-permute-done((bf16[256,1024]{1,0:T(8,128)(2,1)}, bf16[256,1024]{1,0:T(8,128)(2,1)S(1)}, u32[]{:S(2)}, u32[]{:S(2)}) %collective-permute-start.23) | collective-permute-done | bytes 524320 | tf_op jit(solution)/shard_map/ppermute | solution.py:774
  174.7 0.1 add_select_fusion
  174.8 0.8 fusion
  (47 shorter events, 0.1 us)
Async XLA Ops:
  0.6 44.6 %copy-start = (bf16[256,4096]{1,0:T(8,128)(2,1)S(1)}, bf16[256,4096]{1,0:T(8,128)(2,1)}, u32[]{:S(2)}) copy-start(bf16[256,4096]{1,0:T(8,128)(2,1)} %param.15) | copy-start | bytes 6291460
  0.6 44.5 %collective-permute-start = (bf16[512,1024]{1,0:T(8,128)(2,1)}, bf16[512,1024]{1,0:T(8,128)(2,1)}, u32[]{:S(2)}, u32[]{:S(2)}) collective-permute-start(bf16[512,1024]{1,0:T(8,128)(2,1)} %param.14), channel_id=1, source_target_pairs={{0,4},{12,8},{1,5},{13,9},{2,6},{14,10},{3,7},{15,11},{16,20},{28,... | collective-permute-start | bytes 3145736 | tf_op jit(solution)/shard_map/ppermute | solution.py:781
  9.7 35.8 %copy-start.1 = (bf16[256,1536]{1,0:T(8,128)(2,1)}, bf16[256,1536]{1,0:T(8,128)(2,1)S(1)}, u32[]{:S(2)}) copy-start(bf16[256,1536]{1,0:T(8,128)(2,1)S(1)} %constant_dynamic-update-slice_fusion.refs_0_.refs_1_) | copy-start | bytes 2359300
  9.7 8.5 %collective-permute-start.4 = (bf16[256,1536]{1,0:T(8,128)(2,1)S(1)}, bf16[256,1536]{1,0:T(8,128)(2,1)}, u32[]{:S(2)}, u32[]{:S(2)}) collective-permute-start(bf16[256,1536]{1,0:T(8,128)(2,1)S(1)} %constant_dynamic-update-slice_fusion.refs_0_.refs_1_), channel_id=1, source_target_pairs={{12,4},{1,9},{14,6},{3,11},{28,20},{17,25},{30,22},{19,27}} | collective-permute-start | bytes 2359304 | tf_op jit(solution)/shard_map/ppermute | solution.py:779
  11.3 7.0 %collective-permute-start.3 = (bf16[256,1536]{1,0:T(8,128)(2,1)S(1)}, bf16[256,1536]{1,0:T(8,128)(2,1)}, u32[]{:S(2)}, u32[]{:S(2)}) collective-permute-start(bf16[256,1536]{1,0:T(8,128)(2,1)S(1)} %constant_dynamic-update-slice_fusion.refs_0_.refs_1_), channel_id=1, source_target_pairs={{8,4},{5,9},{10,6},{7,11},{24,20},{21,25},{26,22},{23,27}} | collective-permute-start | bytes 2359304 | tf_op jit(solution)/shard_map/ppermute | solution.py:779
  12.8 32.4 %collective-permute-start.2 = (bf16[256,1536]{1,0:T(8,128)(2,1)S(1)}, bf16[256,1536]{1,0:T(8,128)(2,1)}, u32[]{:S(2)}, u32[]{:S(2)}) collective-permute-start(bf16[256,1536]{1,0:T(8,128)(2,1)S(1)} %constant_dynamic-update-slice_fusion.refs_0_.refs_1_), channel_id=1, source_target_pairs={{0,4},{13,9},{2,6},{15,11},{16,20},{29,25},{18,22},{31,27}} | collective-permute-start | bytes 2359304 | tf_op jit(solution)/shard_map/ppermute | solution.py:779
  16.1 2.1 %collective-permute-start.1 = (bf16[256,1024]{1,0:T(8,128)(2,1)S(1)}, bf16[256,1024]{1,0:T(8,128)(2,1)}, u32[]{:S(2)}, u32[]{:S(2)}) collective-permute-start(bf16[256,1024]{1,0:T(8,128)(2,1)S(1)} %constant_dynamic-slice_fusion.4), channel_id=1, source_target_pairs={{8,4},{4,8},{9,5},{5,9},{10,6},{6,10},{11,7},{7,11},{24,20},{20,24... | collective-permute-start | bytes 1572872 | tf_op jit(solution)/shard_map/ppermute | solution.py:789
  45.4 28.4 %collective-permute-start.6 = (bf16[256,1024]{1,0:T(8,128)(2,1)S(1)}, bf16[256,1024]{1,0:T(8,128)(2,1)S(1)}, u32[]{:S(2)}, u32[]{:S(2)}) collective-permute-start(bf16[256,1024]{1,0:T(8,128)(2,1)S(1)} %get-tuple-element.151), channel_id=1, source_target_pairs={{0,4},{12,8},{1,5},{13,9},{2,6},{14,10},{3,7},{15,11},{16,20},{28,... | collective-permute-start | bytes 1572872 | tf_op jit(solution)/shard_map/ppermute | solution.py:789
  51.0 22.8 %collective-permute-start.5 = (bf16[256,1024]{1,0:T(8,128)(2,1)S(1)}, bf16[256,1024]{1,0:T(8,128)(2,1)S(1)}, u32[]{:S(2)}, u32[]{:S(2)}) collective-permute-start(bf16[256,1024]{1,0:T(8,128)(2,1)S(1)} %get-tuple-element.152), channel_id=1, source_target_pairs={{12,4},{0,8},{13,5},{1,9},{14,6},{2,10},{15,7},{3,11},{28,20},{16,... | collective-permute-start | bytes 1572872 | tf_op jit(solution)/shard_map/ppermute | solution.py:789
  52.4 14.1 %copy-start.2 = (bf16[512,1024]{1,0:T(8,128)(2,1)S(1)}, bf16[512,1024]{1,0:T(8,128)(2,1)}, u32[]{:S(2)}) copy-start(bf16[512,1024]{1,0:T(8,128)(2,1)} %param.14) | copy-start | bytes 3145732
  66.4 4.8 %collective-permute-start.7 = (bf16[256,1024]{1,0:T(8,128)(2,1)}, bf16[256,1024]{1,0:T(8,128)(2,1)S(1)}, u32[]{:S(2)}, u32[]{:S(2)}) collective-permute-start(bf16[256,1024]{1,0:T(8,128)(2,1)} %collective-permute-done.1), channel_id=1, source_target_pairs={{0,1},{1,0},{2,3},{3,2},{4,5},{5,4},{6,7},{7,6},{8,9},{9,8},{10,11... | collective-permute-start | bytes 1572872 | tf_op jit(solution)/shard_map/ppermute | solution.py:794
  68.8 2.9 %copy-start.3 = (f32[256,512]{1,0:T(8,128)}, f32[256,512]{1,0:T(8,128)S(1)}, u32[]{:S(2)}) copy-start(f32[256,512]{1,0:T(8,128)S(1)} %convolution_add_fusion.2.refs_2_) | copy-start | bytes 1572868
  68.8 3.6 %copy-start.10 = (f32[8,128]{1,0:T(8,128)S(1)}, f32[8,128]{1,0:T(8,128)}, u32[]{:S(2)}) copy-start(f32[8,128]{1,0:T(8,128)} %get-tuple-element.90) | copy-start | bytes 12292
  68.9 5.0 %collective-permute-start.9 = (f32[256,512]{1,0:T(8,128)S(1)}, f32[256,512]{1,0:T(8,128)S(1)}, u32[]{:S(2)}, u32[]{:S(2)}) collective-permute-start(f32[256,512]{1,0:T(8,128)S(1)} %convolution_add_fusion.2.refs_2_), channel_id=1, source_target_pairs={{8,4},{5,9},{10,6},{7,11},{24,20},{21,25},{26,22},{23,27}} | collective-permute-start | bytes 1572872 | tf_op jit(solution)/shard_map/ppermute | solution.py:843
  71.7 5.2 %copy-start.4 = (f32[256,512]{1,0:T(8,128)}, f32[256,512]{1,0:T(8,128)S(1)}, u32[]{:S(2)}) copy-start(f32[256,512]{1,0:T(8,128)S(1)} %convolution_add_fusion.3.refs_3_) | copy-start | bytes 1572868
  71.7 2.1 %collective-permute-start.8 = (f32[256,512]{1,0:T(8,128)S(1)}, f32[256,512]{1,0:T(8,128)S(1)}, u32[]{:S(2)}, u32[]{:S(2)}) collective-permute-start(f32[256,512]{1,0:T(8,128)S(1)} %convolution_add_fusion.3.refs_3_), channel_id=1, source_target_pairs={{8,4},{5,9},{10,6},{7,11},{24,20},{21,25},{26,22},{23,27}} | collective-permute-start | bytes 1572872 | tf_op jit(solution)/shard_map/ppermute | solution.py:845
  72.4 0.7 collective-permute-start.10
  73.1 3.8 %copy-start.8 = (f32[8,128]{1,0:T(8,128)}, f32[8,128]{1,0:T(8,128)S(1)}, u32[]{:S(2)}) copy-start(f32[8,128]{1,0:T(8,128)S(1)} %add.64.refs_7_.refs_6_) | copy-start | bytes 12292
  73.2 0.7 collective-permute-start.11
  73.9 3.1 %copy-start.12 = (f32[256,512]{1,0:T(8,128)}, f32[256,512]{1,0:T(8,128)S(1)}, u32[]{:S(2)}) copy-start(f32[256,512]{1,0:T(8,128)S(1)} %collective-permute-done.9.refs_5_) | copy-start | bytes 1572868
  73.9 3.1 %copy-start.17 = (f32[8,128]{1,0:T(8,128)}, f32[8,128]{1,0:T(8,128)S(1)}, u32[]{:S(2)}) copy-start(f32[8,128]{1,0:T(8,128)S(1)} %collective-permute-done.11.refs_8_.refs_7_) | copy-start | bytes 12292
  73.9 3.1 %copy-start.13 = (f32[256,512]{1,0:T(8,128)}, f32[256,512]{1,0:T(8,128)S(1)}, u32[]{:S(2)}) copy-start(f32[256,512]{1,0:T(8,128)S(1)} %collective-permute-done.8.refs_4_) | copy-start | bytes 1572868
  73.9 2.1 %collective-permute-start.12 = (bf16[256,1024]{1,0:T(8,128)(2,1)S(1)}, bf16[256,1024]{1,0:T(8,128)(2,1)S(1)}, u32[]{:S(2)}, u32[]{:S(2)}) collective-permute-start(bf16[256,1024]{1,0:T(8,128)(2,1)S(1)} %collective-permute-done.5), channel_id=1, source_target_pairs={{0,1},{1,0},{2,3},{3,2},{4,5},{5,4},{6,7},{7,6},{8,9},{9,8},{10,11... | collective-permute-start | bytes 1572872 | tf_op jit(solution)/shard_map/ppermute | solution.py:794
  74.5 3.3 %collective-permute-start.13 = (bf16[256,1024]{1,0:T(8,128)(2,1)S(1)}, bf16[256,1024]{1,0:T(8,128)(2,1)S(1)}, u32[]{:S(2)}, u32[]{:S(2)}) collective-permute-start(bf16[256,1024]{1,0:T(8,128)(2,1)S(1)} %collective-permute-done.6), channel_id=1, source_target_pairs={{0,1},{1,0},{2,3},{3,2},{4,5},{5,4},{6,7},{7,6},{8,9},{9,8},{10,11... | collective-permute-start | bytes 1572872 | tf_op jit(solution)/shard_map/ppermute | solution.py:794
  77.0 1.7 copy-start.5
  77.0 17.3 %collective-permute-start.14 = (f32[256,512]{1,0:T(8,128)S(1)}, f32[256,512]{1,0:T(8,128)S(1)}, u32[]{:S(2)}, u32[]{:S(2)}) collective-permute-start(f32[256,512]{1,0:T(8,128)S(1)} %convolution_add_fusion.1.refs_3_), channel_id=1, source_target_pairs={{8,4},{5,9},{10,6},{7,11},{24,20},{21,25},{26,22},{23,27}} | collective-permute-start | bytes 1572872 | tf_op jit(solution)/shard_map/ppermute | solution.py:851
  78.7 15.6 %copy-start.6 = (f32[256,512]{1,0:T(8,128)}, f32[256,512]{1,0:T(8,128)S(1)}, u32[]{:S(2)}) copy-start(f32[256,512]{1,0:T(8,128)S(1)} %convolution_add_fusion.refs_2_) | copy-start | bytes 1572868
  78.7 15.6 %collective-permute-start.15 = (f32[256,512]{1,0:T(8,128)S(1)}, f32[256,512]{1,0:T(8,128)S(1)}, u32[]{:S(2)}, u32[]{:S(2)}) collective-permute-start(f32[256,512]{1,0:T(8,128)S(1)} %convolution_add_fusion.refs_2_), channel_id=1, source_target_pairs={{8,4},{5,9},{10,6},{7,11},{24,20},{21,25},{26,22},{23,27}} | collective-permute-start | bytes 1572872 | tf_op jit(solution)/shard_map/ppermute | solution.py:853
  94.3 0.8 copy-start.14
  94.3 1.0 copy-start.15
  106.7 5.8 %collective-permute-start.16 = (f32[8,128]{1,0:T(8,128)}, f32[8,128]{1,0:T(8,128)S(1)}, u32[]{:S(2)}, u32[]{:S(2)}) collective-permute-start(f32[8,128]{1,0:T(8,128)} %get-tuple-element.116), channel_id=1, source_target_pairs={{4,9},{9,4},{6,11},{11,6},{20,25},{25,20},{22,27},{27,22}} | collective-permute-start | bytes 12296 | tf_op jit(solution)/shard_map/ppermute | solution.py:800
  107.3 5.1 %copy-start.11 = (f32[8,128]{1,0:T(8,128)S(1)}, f32[8,128]{1,0:T(8,128)}, u32[]{:S(2)}) copy-start(f32[8,128]{1,0:T(8,128)} %get-tuple-element.116) | copy-start | bytes 12292
  107.3 5.8 %copy-start.16 = (bf16[256,512]{1,0:T(8,128)(2,1)S(1)}, bf16[256,512]{1,0:T(8,128)(2,1)}, u32[]{:S(2)}) copy-start(bf16[256,512]{1,0:T(8,128)(2,1)} %get-tuple-element.126) | copy-start | bytes 786436
  112.4 3.6 %copy-start.9 = (f32[8,128]{1,0:T(8,128)}, f32[8,128]{1,0:T(8,128)S(1)}, u32[]{:S(2)}) copy-start(f32[8,128]{1,0:T(8,128)S(1)} %add.67.refs_8_) | copy-start | bytes 12292
  112.4 1.4 collective-permute-start.17
  113.1 17.1 %collective-permute-start.19 = (bf16[256,512]{1,0:T(8,128)(2,1)S(1)}, bf16[256,512]{1,0:T(8,128)(2,1)S(1)}, u32[]{:S(2)}, u32[]{:S(2)}) collective-permute-start(bf16[256,512]{1,0:T(8,128)(2,1)S(1)} %copy-done.16), channel_id=1, source_target_pairs={{4,8},{9,5},{6,10},{11,7},{20,24},{25,21},{22,26},{27,23}} | collective-permute-start | bytes 786440 | tf_op jit(solution)/shard_map/ppermute | solution.py:774
  113.8 2.2 %copy-start.18 = (f32[8,128]{1,0:T(8,128)}, f32[8,128]{1,0:T(8,128)S(1)}, u32[]{:S(2)}) copy-start(f32[8,128]{1,0:T(8,128)S(1)} %collective-permute-done.17.refs_9_) | copy-start | bytes 12292
  113.8 26.2 %collective-permute-start.18 = (bf16[256,512]{1,0:T(8,128)(2,1)}, bf16[256,512]{1,0:T(8,128)(2,1)S(1)}, u32[]{:S(2)}, u32[]{:S(2)}) collective-permute-start(bf16[256,512]{1,0:T(8,128)(2,1)} %get-tuple-element.125), channel_id=1, source_target_pairs={{4,0},{9,13},{6,2},{11,15},{20,16},{25,29},{22,18},{27,31}} | collective-permute-start | bytes 786440 | tf_op jit(solution)/shard_map/ppermute | solution.py:774
  115.1 24.9 %collective-permute-start.20 = (bf16[256,512]{1,0:T(8,128)(2,1)}, bf16[256,512]{1,0:T(8,128)(2,1)S(1)}, u32[]{:S(2)}, u32[]{:S(2)}) collective-permute-start(bf16[256,512]{1,0:T(8,128)(2,1)} %get-tuple-element.127), channel_id=1, source_target_pairs={{4,12},{9,1},{6,14},{11,3},{20,28},{25,17},{22,30},{27,19}} | collective-permute-start | bytes 786440 | tf_op jit(solution)/shard_map/ppermute | solution.py:774
  116.1 25.3 %copy-start.7 = (bf16[256,512]{1,0:T(8,128)(2,1)S(1)}, bf16[256,512]{1,0:T(8,128)(2,1)}, u32[]{:S(2)}) copy-start(bf16[256,512]{1,0:T(8,128)(2,1)} %get-tuple-element.138) | copy-start | bytes 786436
  140.0 16.3 %collective-permute-start.21 = (bf16[256,1024]{1,0:T(8,128)(2,1)}, bf16[256,1024]{1,0:T(8,128)(2,1)S(1)}, u32[]{:S(2)}, u32[]{:S(2)}) collective-permute-start(bf16[256,1024]{1,0:T(8,128)(2,1)} %get-tuple-element.128), channel_id=1, source_target_pairs={{4,12},{9,1},{6,14},{11,3},{20,28},{25,17},{22,30},{27,19}} | collective-permute-start | bytes 1572872 | tf_op jit(solution)/shard_map/ppermute | solution.py:774
  140.7 15.7 %collective-permute-start.22 = (bf16[256,1024]{1,0:T(8,128)(2,1)}, bf16[256,1024]{1,0:T(8,128)(2,1)S(1)}, u32[]{:S(2)}, u32[]{:S(2)}) collective-permute-start(bf16[256,1024]{1,0:T(8,128)(2,1)} %get-tuple-element.129), channel_id=1, source_target_pairs={{4,8},{9,5},{6,10},{11,7},{20,24},{25,21},{22,26},{27,23}} | collective-permute-start | bytes 1572872 | tf_op jit(solution)/shard_map/ppermute | solution.py:774
  156.4 18.3 %collective-permute-start.23 = (bf16[256,1024]{1,0:T(8,128)(2,1)}, bf16[256,1024]{1,0:T(8,128)(2,1)S(1)}, u32[]{:S(2)}, u32[]{:S(2)}) collective-permute-start(bf16[256,1024]{1,0:T(8,128)(2,1)} %get-tuple-element.144), channel_id=1, source_target_pairs={{4,0},{9,13},{6,2},{11,15},{20,16},{25,29},{22,18},{27,31}} | collective-permute-start | bytes 1572872 | tf_op jit(solution)/shard_map/ppermute | solution.py:774

commit v3 on v2

--- a/solution.py
+++ b/solution.py
@@ -778,7 +778,12 @@
     rows_in = jnp.concatenate([keys, values, queries], axis=1)
     slots = [rows_in] + [lax.ppermute(rows_in, both, to_root(j)) for j in range(1, toks)]
 
-    far = lax.ppermute(out_proj, "tok", [(0, low), (3, high)])
+    group, half = lax.axis_index("groups"), out_proj.shape[0] // 2
+    far_half = lax.ppermute(
+        lax.dynamic_slice_in_dim(out_proj, group * half, half, axis=0),
+        "tok",
+        [(0, low), (3, high)],
+    )
     quarter = grad_out.shape[1] // 4
 
     def columns(array, which, half_is_low):
@@ -794,7 +799,8 @@
         return lax.ppermute(value, "head", [(h, h ^ 1) for h in range(heads)])
 
     piece2 = piece(grad_out, 2)
-    later, far, piece2, *slots = tie((grad_out, far, piece2, *slots))
+    later, far_half, piece2, *slots = tie((grad_out, far_half, piece2, *slots))
+    far_other = lax.ppermute(far_half, "groups", [(0, 1), (1, 0)])
 
     def exchange(value, pairs, step_pairs, beside=None):
         more = lax.ppermute(value, both, pairs)
@@ -822,17 +828,23 @@
     piece3 = piece(later, 3)
     piece1 = piece(later, 1)
     g, squares, kept = call_gradient(slots, key_gain, wa, wb)
-    g, squares, far, piece2, mine0, theirs0 = tie(
+    g, squares, far_half, far_other, piece2, mine0, theirs0 = tie(
         (
             g,
             squares,
-            far,
+            far_half,
+            far_other,
             piece2,
             columns(later, core, at_low),
             columns(later, 1 - core, at_low),
         )
     )
 
+    far = jnp.where(
+        group == 0,
+        jnp.concatenate([far_half, far_other], axis=0),
+        jnp.concatenate([far_other, far_half], axis=0),
+    )
     w_mine = jnp.where(core == 0, out_proj, far)
     w_theirs = jnp.where(core == 0, far, out_proj)
 
@@ -882,7 +894,7 @@
 
 
 def per_device(*arrays):
-    fits = lax.axis_size("tok") == 4 and lax.axis_size("head") >= 4
+    fits = lax.axis_size("tok") == 4 and lax.axis_size("head") >= 4 and lax.axis_size("groups") == 2
     return (four_line if fits else any_line)(*arrays)
 
 

time: 177 us -> 173 us (0.977)
  waiting for transfers between devices: 55.3 us -> 45.9 us
  starting transfers between devices: 31.8 us -> 35.7 us
  local copies, waits for them, and re-layouts: 6.08 us -> 8.1 us
    ppermute x3, waiting for transfers between devices: 27 us -> 0.01 us  [four_line(): lax.ppermute(rows_in, both, to_root(j))]
    ppermute x1 -> x2, waiting for transfers between devices: 0.01 us -> 15.7 us  [the longest x1 15.7 us: four_line(): lax.ppermute(lax.dynamic_slice_in_dim(out_proj, group * half, half, axis=...]
    ppermute x3, starting transfers between devices: 5.31 us -> 8.42 us  [four_line(): lax.ppermute(rows_in, both, to_root(j))]
    ppermute x6, waiting for transfers between devices: 26.8 us -> 28.7 us  [home(): return lax.ppermute(value, both, [(b, a) for a, b in to_root(j)])]
    ppermute x1 -> x2, starting transfers between devices: 6.09 us -> 7.82 us  [the longest x1 6.24 us: four_line(): lax.ppermute(lax.dynamic_slice_in_dim(out_proj, group * half, half, axis=...]
  transfers between devices with their start and end apart: 24 -> 25, of which waited for: 4 -> 4; matrix products, arithmetic and copies ran while one was open for 6% -> 6% of each run, Pallas kernels for 35% -> 36%
where the time goes in v3:
time: 173 us; the launch traced here: 172 us
  Pallas kernels  73.4 us (42%)
  waiting for transfers between devices  45.9 us (27%)
  starting transfers between devices  35.7 us (21%)
  local copies, waits for them, and re-layouts  8.1 us (5%)
  matrix products  3.78 us (2%)
  other arithmetic  3.31 us (2%)
  between operations  2 us (1%)
    pallas_call x6, Pallas kernels, call(): pl.pallas_call(kernel, out_shape=out_shape, in_specs=[spec for _, spec in...  73.4 us
    ppermute x6, waiting for transfers between devices, home(): return lax.ppermute(value, both, [(b, a) for a, b in to_root(j)])  28.7 us
    ppermute x1, waiting for transfers between devices, four_line(): lax.ppermute(lax.dynamic_slice_in_dim(out_proj, group * half, half, axis=...  15.7 us
    ppermute x3, starting transfers between devices, four_line(): lax.ppermute(rows_in, both, to_root(j))  8.42 us
    ppermute x3, starting transfers between devices, piece(): lax.ppermute(columns(array, core, place == line[j]), 'tok', [(line[j], lo...  7.44 us
    ppermute x1, starting transfers between devices, four_line(): lax.ppermute(lax.dynamic_slice_in_dim(out_proj, group * half, half, axis=...  6.24 us
    ppermute x6, starting transfers between devices, home(): return lax.ppermute(value, both, [(b, a) for a, b in to_root(j)])  5.54 us
    dot_general x8, matrix products, nt(): lax.dot_general(a, b, (((1,), (1,)), ((), ())), preferred_element_type=f32)  3.78 us
  transfers between devices with their start and end apart: 25, of which 4 were waited for; matrix products, arithmetic and copies ran while one was open for 6% of the time, Pallas kernels for 36%

profile of v3, /device:TPU:0, one launch (start us, length us, event | category | flops | bytes accessed | tf_op | source)
XLA Modules:
  0.0 172.1 jit_solution(10209158388665620854)
XLA Ops:
  0.6 0.0 copy-start
  0.6 1.1 constant_dynamic-update-slice_fusion.2
  1.8 1.0 constant_dynamic-update-slice_fusion.1
  2.7 1.0 constant_dynamic-update-slice_fusion.refs_0_.refs_1_
  3.7 1.6 collective-permute-start.4
  5.3 1.5 collective-permute-start.3
  6.9 5.3 %collective-permute-start.2 = (bf16[256,1536]{1,0:T(8,128)(2,1)S(1)}, bf16[256,1536]{1,0:T(8,128)(2,1)}, u32[]{:S(2)}, u32[]{:S(2)}) collective-permute-start(bf16[256,1536]{1,0:T(8,128)(2,1)S(1)} %constant_dynamic-update-slice_fusion.refs_0_.refs_1_), channel_id=1, source_target_pairs={{0,4},{13,9},{2,6},{15,11},{16,20},{29,25},{18,22},{31,27}} | collective-permute-start | bytes 2359304 | tf_op jit(solution)/shard_map/ppermute | solution.py:779
  12.1 1.9 %constant_dynamic-slice_fusion.4 = bf16[256,1024]{1,0:T(8,128)(2,1)} fusion(bf16[256,4096]{1,0:T(8,128)(2,1)} %param.15, s32[]{:T(128)S(6)} %select_n.74), kind=kLoop, calls=%fused_computation.16 | loop fusion | bytes 1048580 | tf_op jit(solution)/shard_map/dynamic_slice | solution.py:791
  14.0 0.7 collective-permute-start.1
  14.7 1.1 constant_dynamic-slice_fusion.5
  15.8 6.2 %collective-permute-start = (bf16[256,1024]{1,0:T(8,128)(2,1)S(1)}, bf16[256,1024]{1,0:T(8,128)(2,1)}, u32[]{:S(2)}, u32[]{:S(2)}) collective-permute-start(bf16[256,1024]{1,0:T(8,128)(2,1)S(1)} %constant_dynamic-slice_fusion.5), channel_id=1, source_target_pairs={{0,4},{12,8},{1,5},{13,9},{2,6},{14,10},{3,7},{15,11},{16,20},{28,... | collective-permute-start | bytes 1572872 | tf_op jit(solution)/shard_map/ppermute | solution.py:782
  22.0 15.7 %collective-permute-done = bf16[256,1024]{1,0:T(8,128)(2,1)} collective-permute-done((bf16[256,1024]{1,0:T(8,128)(2,1)S(1)}, bf16[256,1024]{1,0:T(8,128)(2,1)}, u32[]{:S(2)}, u32[]{:S(2)}) %collective-permute-start) | collective-permute-done | bytes 524320 | tf_op jit(solution)/shard_map/ppermute | solution.py:782
  37.7 0.0 collective-permute-done.4.refs_3_.refs_1_.refs_0_
  37.7 0.0 collective-permute-done.3.refs_2_.refs_1_
  37.7 0.0 collective-permute-done.2.refs_1_.refs_0_
  37.7 1.6 collective-permute-start.7
  40.0 0.2 constant_dynamic-slice_fusion
  40.2 5.4 %collective-permute-start.6 = (bf16[256,1024]{1,0:T(8,128)(2,1)S(1)}, bf16[256,1024]{1,0:T(8,128)(2,1)S(1)}, u32[]{:S(2)}, u32[]{:S(2)}) collective-permute-start(bf16[256,1024]{1,0:T(8,128)(2,1)S(1)} %get-tuple-element.153), channel_id=1, source_target_pairs={{0,4},{12,8},{1,5},{13,9},{2,6},{14,10},{3,7},{15,11},{16,20},{28,... | collective-permute-start | bytes 1572872 | tf_op jit(solution)/shard_map/ppermute | solution.py:794
  45.7 1.3 collective-permute-start.5
  47.0 0.0 copy-start.1
  47.0 14.0 %gradient.1 = (f32[512,1536]{1,0:T(8,128)}, f32[8,128]{1,0:T(8,128)}, f32[1024,1024]{1,0:T(8,128)}) custom-call(bf16[256,1536]{1,0:T(8,128)(2,1)} %copy-done.2, bf16[256,1536]{1,0:T(8,128)(2,1)} %collective-permute-done.2.refs_1_.refs_0_, bf16[256,1536]{1,0:T(8,128)(2,1)} %collective-permute-done.3.refs_2_.refs_1_, ...), custom_call_target="tpu_custom_call" | custom-call | flops 5368709 | bytes 1048576 | tf_op jit(solution)/shard_map/gradient/pallas_call | solution.py:475
  61.1 0.1 collective-permute-start.8
  61.2 2.4 %broadcast_select_fusion.1 = (bf16[512,1024]{1,0:T(8,128)(2,1)S(1)}, bf16[512,1024]{1,0:T(8,128)(2,1)S(1)}) fusion(bf16[512,1024]{1,0:T(8,128)(2,1)S(1)} %copy-done.1, pred[]{:T(512)S(6)} %eq.23, bf16[256,1024]{1,0:T(8,128)(2,1)} %collective-permute-done, bf16[256,1024]{1,0:T(8,128)(2,1)} %collective-permute-done.7, pred[]{:T(512)S(6)} %eq.24), kind=kLoop, calls=%fused_computation.6 | loop fusion | flops 5767168 | bytes 4194306 | tf_op jit(solution)/shard_map/jit(_where)/select_n | solution.py:848
  63.6 0.5 fusion.2
  64.1 0.5 convolution_add_fusion.2.refs_2_
  64.6 0.0 copy-start.10
  64.6 0.8 collective-permute-start.10
  65.4 0.5 fusion.1
  65.9 0.5 convolution_add_fusion.3.refs_3_
  66.4 0.7 collective-permute-start.9
  67.1 0.7 collective-permute-start.11
  67.8 0.7 collective-permute-start.12
  68.6 0.6 collective-permute-start.13
  69.1 0.1 collective-permute-start.14
  69.2 1.5 collective-permute-done.13
  70.7 0.5 fusion.3
  71.2 0.5 convolution_add_fusion.1.refs_3_
  71.7 0.7 collective-permute-start.15
  72.4 0.5 fusion.4
  72.9 0.5 convolution_add_fusion.refs_2_
  73.4 0.9 collective-permute-start.16
  74.3 14.7 %query_pull.2 = (f32[512,1536]{1,0:T(8,128)}, bf16[512,1536]{1,0:T(8,128)(2,1)}, bf16[512,1536]{1,0:T(8,128)(2,1)}, bf16[256,512]{1,0:T(8,128)(2,1)}, bf16[256,512]{1,0:T(8,128)(2,1)}) custom-call(bf16[256,1536]{1,0:T(8,128)(2,1)} %copy-done.2, bf16[256,1536]{1,0:T(8,128)(2,1)} %collective-permute-done.3.refs_2_.refs_1_, f32[256,512]{1,0:T(8,128)} %copy-done.3, ...), custom_call_target="tpu_custom_call" | custom-call | flops 5368709120 | bytes 1048576 | tf_op jit(solution)/shard_map/query_pull/pallas_call | solution.py:475
  89.0 0.8 copy-done.14
  89.8 0.2 copy-done.15
  89.9 11.4 %query_pull.3 = (f32[512,1536]{1,0:T(8,128)}, f32[8,128]{1,0:T(8,128)}, bf16[512,1024]{1,0:T(8,128)(2,1)}, bf16[512,1024]{1,0:T(8,128)(2,1)}) custom-call(bf16[256,1536]{1,0:T(8,128)(2,1)} %collective-permute-done.2.refs_1_.refs_0_, bf16[256,1536]{1,0:T(8,128)(2,1)} %collective-permute-done.4.refs_3_.refs_1_.refs_0_, f32[256,512]{1,0:T(8,128)} %copy-done.6, ...), custom_call_target="tpu_custom_call" | custom-call | flops 5368709120 | bytes 1048576 | tf_op jit(solution)/shard_map/query_pull/pallas_call | solution.py:475
  101.3 0.7 collective-permute-start.17
  102.0 0.0 copy-start.16
  102.0 5.1 %query_grad.1 = (bf16[256,512]{1,0:T(8,128)(2,1)}, bf16[256,512]{1,0:T(8,128)(2,1)}) custom-call(bf16[512,1024]{1,0:T(8,128)(2,1)} %get-tuple-element.114.mh, bf16[512,1024]{1,0:T(8,128)(2,1)} %get-tuple-element.115.ml, bf16[512,1536]{1,0:T(8,128)(2,1)} %get-tuple-element.111.refs_8_.uh, bf16[512,1536]{1,0:T(8,128)(2,1)} %get-tuple-element.112.refs_9_.ul), custom_call_target="tpu_custom_call" | custom-call | flops 1610612736 | bytes 1048576 | tf_op jit(solution)/shard_map/query_grad/pallas_call | solution.py:475
  107.1 0.7 collective-permute-start.18
  107.8 0.7 collective-permute-start.20
  108.5 0.0 copy-start.18
  108.5 1.3 collective-permute-start.19
  109.8 0.9 collective-permute-start.21
  110.7 0.0 copy-start.7
  110.7 14.1 %key_pull.2 = (bf16[256,1024]{1,0:T(8,128)(2,1)}, bf16[256,1024]{1,0:T(8,128)(2,1)}) custom-call(bf16[256,1536]{1,0:T(8,128)(2,1)} %collective-permute-done.4.refs_3_.refs_1_.refs_0_, bf16[256,1536]{1,0:T(8,128)(2,1)} %collective-permute-done.3.refs_2_.refs_1_, f32[1024,1024]{1,0:T(8,128)} %get-tuple-element.80.refs_2_, f32[1]{0:T(128)S(6)} %copy.13.refs_4_.refs_3_, ...), custom_call_target="tpu_custom_call" | custom-call | flops 6979321856 | bytes 1048576 | tf_op jit(solution)/shard_map/key_pull/pallas_call | solution.py:475
  124.9 11.7 %collective-permute-done.19 = bf16[256,512]{1,0:T(8,128)(2,1)S(1)} collective-permute-done((bf16[256,512]{1,0:T(8,128)(2,1)}, bf16[256,512]{1,0:T(8,128)(2,1)S(1)}, u32[]{:S(2)}, u32[]{:S(2)}) %collective-permute-start.19) | collective-permute-done | bytes 262176 | tf_op jit(solution)/shard_map/ppermute | solution.py:774
  136.5 0.7 collective-permute-start.22
  137.2 0.7 collective-permute-start.23
  137.9 0.8 add_select_fusion.1
  138.7 14.2 %key_pull.3 = (bf16[256,1024]{1,0:T(8,128)(2,1)}, bf16[256,1024]{1,0:T(8,128)(2,1)}) custom-call(bf16[256,1536]{1,0:T(8,128)(2,1)} %collective-permute-done.2.refs_1_.refs_0_, bf16[256,1536]{1,0:T(8,128)(2,1)} %copy-done.2, f32[1024,1024]{1,0:T(8,128)} %get-tuple-element.80.refs_2_, f32[1]{0:T(128)S(6)} %copy.13.refs_4_.refs_3_, bf16[512,1024]{1,0:T(8,128)(2,1)} %bitcast.21, ...), custom_call_target="tpu_custom_call" | custom-call | flops 6979321856 | bytes 1048576 | tf_op jit(solution)/shard_map/key_pull/pallas_call | solution.py:475
  152.9 1.3 collective-permute-start.24
  154.2 17.0 %collective-permute-done.24 = bf16[256,1024]{1,0:T(8,128)(2,1)S(1)} collective-permute-done((bf16[256,1024]{1,0:T(8,128)(2,1)}, bf16[256,1024]{1,0:T(8,128)(2,1)S(1)}, u32[]{:S(2)}, u32[]{:S(2)}) %collective-permute-start.24) | collective-permute-done | bytes 524320 | tf_op jit(solution)/shard_map/ppermute | solution.py:774
  171.2 0.1 add_select_fusion
  171.3 0.8 fusion
  (50 shorter events, 0.1 us)
Async XLA Ops:
  0.6 39.4 %copy-start = (bf16[256,4096]{1,0:T(8,128)(2,1)S(1)}, bf16[256,4096]{1,0:T(8,128)(2,1)}, u32[]{:S(2)}) copy-start(bf16[256,4096]{1,0:T(8,128)(2,1)} %param.15) | copy-start | bytes 6291460
  3.7 36.5 %copy-start.2 = (bf16[256,1536]{1,0:T(8,128)(2,1)}, bf16[256,1536]{1,0:T(8,128)(2,1)S(1)}, u32[]{:S(2)}) copy-start(bf16[256,1536]{1,0:T(8,128)(2,1)S(1)} %constant_dynamic-update-slice_fusion.refs_0_.refs_1_) | copy-start | bytes 2359300
  3.7 34.0 %collective-permute-start.4 = (bf16[256,1536]{1,0:T(8,128)(2,1)S(1)}, bf16[256,1536]{1,0:T(8,128)(2,1)}, u32[]{:S(2)}, u32[]{:S(2)}) collective-permute-start(bf16[256,1536]{1,0:T(8,128)(2,1)S(1)} %constant_dynamic-update-slice_fusion.refs_0_.refs_1_), channel_id=1, source_target_pairs={{12,4},{1,9},{14,6},{3,11},{28,20},{17,25},{30,22},{19,27}} | collective-permute-start | bytes 2359304 | tf_op jit(solution)/shard_map/ppermute | solution.py:779
  5.3 32.4 %collective-permute-start.3 = (bf16[256,1536]{1,0:T(8,128)(2,1)S(1)}, bf16[256,1536]{1,0:T(8,128)(2,1)}, u32[]{:S(2)}, u32[]{:S(2)}) collective-permute-start(bf16[256,1536]{1,0:T(8,128)(2,1)S(1)} %constant_dynamic-update-slice_fusion.refs_0_.refs_1_), channel_id=1, source_target_pairs={{8,4},{5,9},{10,6},{7,11},{24,20},{21,25},{26,22},{23,27}} | collective-permute-start | bytes 2359304 | tf_op jit(solution)/shard_map/ppermute | solution.py:779
  6.9 30.9 %collective-permute-start.2 = (bf16[256,1536]{1,0:T(8,128)(2,1)S(1)}, bf16[256,1536]{1,0:T(8,128)(2,1)}, u32[]{:S(2)}, u32[]{:S(2)}) collective-permute-start(bf16[256,1536]{1,0:T(8,128)(2,1)S(1)} %constant_dynamic-update-slice_fusion.refs_0_.refs_1_), channel_id=1, source_target_pairs={{0,4},{13,9},{2,6},{15,11},{16,20},{29,25},{18,22},{31,27}} | collective-permute-start | bytes 2359304 | tf_op jit(solution)/shard_map/ppermute | solution.py:779
  14.0 8.0 %collective-permute-start.1 = (bf16[256,1024]{1,0:T(8,128)(2,1)}, bf16[256,1024]{1,0:T(8,128)(2,1)S(1)}, u32[]{:S(2)}, u32[]{:S(2)}) collective-permute-start(bf16[256,1024]{1,0:T(8,128)(2,1)} %constant_dynamic-slice_fusion.4), channel_id=1, source_target_pairs={{8,4},{4,8},{9,5},{5,9},{10,6},{6,10},{11,7},{7,11},{24,20},{20,24... | collective-permute-start | bytes 1572872 | tf_op jit(solution)/shard_map/ppermute | solution.py:794
  15.8 21.9 %collective-permute-start = (bf16[256,1024]{1,0:T(8,128)(2,1)S(1)}, bf16[256,1024]{1,0:T(8,128)(2,1)}, u32[]{:S(2)}, u32[]{:S(2)}) collective-permute-start(bf16[256,1024]{1,0:T(8,128)(2,1)S(1)} %constant_dynamic-slice_fusion.5), channel_id=1, source_target_pairs={{0,4},{12,8},{1,5},{13,9},{2,6},{14,10},{3,7},{15,11},{16,20},{28,... | collective-permute-start | bytes 1572872 | tf_op jit(solution)/shard_map/ppermute | solution.py:782
  37.7 23.3 %collective-permute-start.7 = (bf16[256,1024]{1,0:T(8,128)(2,1)}, bf16[256,1024]{1,0:T(8,128)(2,1)}, u32[]{:S(2)}, u32[]{:S(2)}) collective-permute-start(bf16[256,1024]{1,0:T(8,128)(2,1)} %collective-permute-done), channel_id=1, source_target_pairs={{0,16},{16,0},{1,17},{17,1},{2,18},{18,2},{3,19},{19,3},{4,20},{20... | collective-permute-start | bytes 1572872 | tf_op jit(solution)/shard_map/ppermute | solution.py:803
  40.2 28.3 %collective-permute-start.6 = (bf16[256,1024]{1,0:T(8,128)(2,1)S(1)}, bf16[256,1024]{1,0:T(8,128)(2,1)S(1)}, u32[]{:S(2)}, u32[]{:S(2)}) collective-permute-start(bf16[256,1024]{1,0:T(8,128)(2,1)S(1)} %get-tuple-element.153), channel_id=1, source_target_pairs={{0,4},{12,8},{1,5},{13,9},{2,6},{14,10},{3,7},{15,11},{16,20},{28,... | collective-permute-start | bytes 1572872 | tf_op jit(solution)/shard_map/ppermute | solution.py:794
  45.7 22.8 %collective-permute-start.5 = (bf16[256,1024]{1,0:T(8,128)(2,1)S(1)}, bf16[256,1024]{1,0:T(8,128)(2,1)S(1)}, u32[]{:S(2)}, u32[]{:S(2)}) collective-permute-start(bf16[256,1024]{1,0:T(8,128)(2,1)S(1)} %get-tuple-element.154), channel_id=1, source_target_pairs={{12,4},{0,8},{13,5},{1,9},{14,6},{2,10},{15,7},{3,11},{28,20},{16,... | collective-permute-start | bytes 1572872 | tf_op jit(solution)/shard_map/ppermute | solution.py:794
  47.0 14.1 %copy-start.1 = (bf16[512,1024]{1,0:T(8,128)(2,1)S(1)}, bf16[512,1024]{1,0:T(8,128)(2,1)}, u32[]{:S(2)}) copy-start(bf16[512,1024]{1,0:T(8,128)(2,1)} %param.14) | copy-start | bytes 3145732
  61.1 4.4 %collective-permute-start.8 = (bf16[256,1024]{1,0:T(8,128)(2,1)S(1)}, bf16[256,1024]{1,0:T(8,128)(2,1)S(1)}, u32[]{:S(2)}, u32[]{:S(2)}) collective-permute-start(bf16[256,1024]{1,0:T(8,128)(2,1)S(1)} %collective-permute-done.1), channel_id=1, source_target_pairs={{0,1},{1,0},{2,3},{3,2},{4,5},{5,4},{6,7},{7,6},{8,9},{9,8},{10,11... | collective-permute-start | bytes 1572872 | tf_op jit(solution)/shard_map/ppermute | solution.py:799
  64.6 1.8 %copy-start.3 = (f32[256,512]{1,0:T(8,128)}, f32[256,512]{1,0:T(8,128)S(1)}, u32[]{:S(2)}) copy-start(f32[256,512]{1,0:T(8,128)S(1)} %convolution_add_fusion.2.refs_2_) | copy-start | bytes 1572868
  64.6 2.5 %copy-start.10 = (f32[8,128]{1,0:T(8,128)S(1)}, f32[8,128]{1,0:T(8,128)}, u32[]{:S(2)}) copy-start(f32[8,128]{1,0:T(8,128)} %get-tuple-element.92) | copy-start | bytes 12292
  64.6 3.9 %collective-permute-start.10 = (f32[256,512]{1,0:T(8,128)S(1)}, f32[256,512]{1,0:T(8,128)S(1)}, u32[]{:S(2)}, u32[]{:S(2)}) collective-permute-start(f32[256,512]{1,0:T(8,128)S(1)} %convolution_add_fusion.2.refs_2_), channel_id=1, source_target_pairs={{8,4},{5,9},{10,6},{7,11},{24,20},{21,25},{26,22},{23,27}} | collective-permute-start | bytes 1572872 | tf_op jit(solution)/shard_map/ppermute | solution.py:855
  66.4 5.2 %copy-start.4 = (f32[256,512]{1,0:T(8,128)}, f32[256,512]{1,0:T(8,128)S(1)}, u32[]{:S(2)}) copy-start(f32[256,512]{1,0:T(8,128)S(1)} %convolution_add_fusion.3.refs_3_) | copy-start | bytes 1572868
  66.4 2.1 %collective-permute-start.9 = (f32[256,512]{1,0:T(8,128)S(1)}, f32[256,512]{1,0:T(8,128)S(1)}, u32[]{:S(2)}, u32[]{:S(2)}) collective-permute-start(f32[256,512]{1,0:T(8,128)S(1)} %convolution_add_fusion.3.refs_3_), channel_id=1, source_target_pairs={{8,4},{5,9},{10,6},{7,11},{24,20},{21,25},{26,22},{23,27}} | collective-permute-start | bytes 1572872 | tf_op jit(solution)/shard_map/ppermute | solution.py:857
  67.1 0.7 collective-permute-start.11
  67.8 3.8 %copy-start.8 = (f32[8,128]{1,0:T(8,128)}, f32[8,128]{1,0:T(8,128)S(1)}, u32[]{:S(2)}) copy-start(f32[8,128]{1,0:T(8,128)S(1)} %add.68.refs_7_.refs_6_) | copy-start | bytes 12292
  67.8 0.7 collective-permute-start.12
  68.5 3.1 %copy-start.12 = (f32[256,512]{1,0:T(8,128)}, f32[256,512]{1,0:T(8,128)S(1)}, u32[]{:S(2)}) copy-start(f32[256,512]{1,0:T(8,128)S(1)} %collective-permute-done.10.refs_5_) | copy-start | bytes 1572868
  68.6 3.1 %copy-start.17 = (f32[8,128]{1,0:T(8,128)}, f32[8,128]{1,0:T(8,128)S(1)}, u32[]{:S(2)}) copy-start(f32[8,128]{1,0:T(8,128)S(1)} %collective-permute-done.12.refs_8_.refs_7_) | copy-start | bytes 12292
  68.6 3.1 %copy-start.13 = (f32[256,512]{1,0:T(8,128)}, f32[256,512]{1,0:T(8,128)S(1)}, u32[]{:S(2)}) copy-start(f32[256,512]{1,0:T(8,128)S(1)} %collective-permute-done.9.refs_4_) | copy-start | bytes 1572868
  68.6 2.1 %collective-permute-start.13 = (bf16[256,1024]{1,0:T(8,128)(2,1)S(1)}, bf16[256,1024]{1,0:T(8,128)(2,1)S(1)}, u32[]{:S(2)}, u32[]{:S(2)}) collective-permute-start(bf16[256,1024]{1,0:T(8,128)(2,1)S(1)} %collective-permute-done.5), channel_id=1, source_target_pairs={{0,1},{1,0},{2,3},{3,2},{4,5},{5,4},{6,7},{7,6},{8,9},{9,8},{10,11... | collective-permute-start | bytes 1572872 | tf_op jit(solution)/shard_map/ppermute | solution.py:799
  69.1 3.3 %collective-permute-start.14 = (bf16[256,1024]{1,0:T(8,128)(2,1)S(1)}, bf16[256,1024]{1,0:T(8,128)(2,1)S(1)}, u32[]{:S(2)}, u32[]{:S(2)}) collective-permute-start(bf16[256,1024]{1,0:T(8,128)(2,1)S(1)} %collective-permute-done.6), channel_id=1, source_target_pairs={{0,1},{1,0},{2,3},{3,2},{4,5},{5,4},{6,7},{7,6},{8,9},{9,8},{10,11... | collective-permute-start | bytes 1572872 | tf_op jit(solution)/shard_map/ppermute | solution.py:799
  71.7 1.7 copy-start.5
  71.7 17.3 %collective-permute-start.15 = (f32[256,512]{1,0:T(8,128)S(1)}, f32[256,512]{1,0:T(8,128)S(1)}, u32[]{:S(2)}, u32[]{:S(2)}) collective-permute-start(f32[256,512]{1,0:T(8,128)S(1)} %convolution_add_fusion.1.refs_3_), channel_id=1, source_target_pairs={{8,4},{5,9},{10,6},{7,11},{24,20},{21,25},{26,22},{23,27}} | collective-permute-start | bytes 1572872 | tf_op jit(solution)/shard_map/ppermute | solution.py:863
  73.4 15.6 %copy-start.6 = (f32[256,512]{1,0:T(8,128)}, f32[256,512]{1,0:T(8,128)S(1)}, u32[]{:S(2)}) copy-start(f32[256,512]{1,0:T(8,128)S(1)} %convolution_add_fusion.refs_2_) | copy-start | bytes 1572868
  73.4 15.6 %collective-permute-start.16 = (f32[256,512]{1,0:T(8,128)S(1)}, f32[256,512]{1,0:T(8,128)S(1)}, u32[]{:S(2)}, u32[]{:S(2)}) collective-permute-start(f32[256,512]{1,0:T(8,128)S(1)} %convolution_add_fusion.refs_2_), channel_id=1, source_target_pairs={{8,4},{5,9},{10,6},{7,11},{24,20},{21,25},{26,22},{23,27}} | collective-permute-start | bytes 1572872 | tf_op jit(solution)/shard_map/ppermute | solution.py:865
  89.0 0.8 copy-start.14
  89.0 1.0 copy-start.15
  101.3 5.8 %collective-permute-start.17 = (f32[8,128]{1,0:T(8,128)}, f32[8,128]{1,0:T(8,128)S(1)}, u32[]{:S(2)}, u32[]{:S(2)}) collective-permute-start(f32[8,128]{1,0:T(8,128)} %get-tuple-element.118), channel_id=1, source_target_pairs={{4,9},{9,4},{6,11},{11,6},{20,25},{25,20},{22,27},{27,22}} | collective-permute-start | bytes 12296 | tf_op jit(solution)/shard_map/ppermute | solution.py:806
  102.0 5.1 %copy-start.11 = (f32[8,128]{1,0:T(8,128)S(1)}, f32[8,128]{1,0:T(8,128)}, u32[]{:S(2)}) copy-start(f32[8,128]{1,0:T(8,128)} %get-tuple-element.118) | copy-start | bytes 12292
  102.0 5.8 %copy-start.16 = (bf16[256,512]{1,0:T(8,128)(2,1)S(1)}, bf16[256,512]{1,0:T(8,128)(2,1)}, u32[]{:S(2)}) copy-start(bf16[256,512]{1,0:T(8,128)(2,1)} %get-tuple-element.128) | copy-start | bytes 786436
  107.1 3.6 %copy-start.9 = (f32[8,128]{1,0:T(8,128)}, f32[8,128]{1,0:T(8,128)S(1)}, u32[]{:S(2)}) copy-start(f32[8,128]{1,0:T(8,128)S(1)} %add.71.refs_8_) | copy-start | bytes 12292
  107.1 1.4 collective-permute-start.18
  107.8 17.1 %collective-permute-start.20 = (bf16[256,512]{1,0:T(8,128)(2,1)S(1)}, bf16[256,512]{1,0:T(8,128)(2,1)S(1)}, u32[]{:S(2)}, u32[]{:S(2)}) collective-permute-start(bf16[256,512]{1,0:T(8,128)(2,1)S(1)} %copy-done.16), channel_id=1, source_target_pairs={{4,8},{9,5},{6,10},{11,7},{20,24},{25,21},{22,26},{27,23}} | collective-permute-start | bytes 786440 | tf_op jit(solution)/shard_map/ppermute | solution.py:774
  108.5 2.2 %copy-start.18 = (f32[8,128]{1,0:T(8,128)}, f32[8,128]{1,0:T(8,128)S(1)}, u32[]{:S(2)}) copy-start(f32[8,128]{1,0:T(8,128)S(1)} %collective-permute-done.18.refs_9_) | copy-start | bytes 12292
  108.5 28.0 %collective-permute-start.19 = (bf16[256,512]{1,0:T(8,128)(2,1)}, bf16[256,512]{1,0:T(8,128)(2,1)S(1)}, u32[]{:S(2)}, u32[]{:S(2)}) collective-permute-start(bf16[256,512]{1,0:T(8,128)(2,1)} %get-tuple-element.127), channel_id=1, source_target_pairs={{4,0},{9,13},{6,2},{11,15},{20,16},{25,29},{22,18},{27,31}} | collective-permute-start | bytes 786440 | tf_op jit(solution)/shard_map/ppermute | solution.py:774
  109.8 26.7 %collective-permute-start.21 = (bf16[256,512]{1,0:T(8,128)(2,1)}, bf16[256,512]{1,0:T(8,128)(2,1)S(1)}, u32[]{:S(2)}, u32[]{:S(2)}) collective-permute-start(bf16[256,512]{1,0:T(8,128)(2,1)} %get-tuple-element.129), channel_id=1, source_target_pairs={{4,12},{9,1},{6,14},{11,3},{20,28},{25,17},{22,30},{27,19}} | collective-permute-start | bytes 786440 | tf_op jit(solution)/shard_map/ppermute | solution.py:774
  110.7 27.2 %copy-start.7 = (bf16[256,512]{1,0:T(8,128)(2,1)S(1)}, bf16[256,512]{1,0:T(8,128)(2,1)}, u32[]{:S(2)}) copy-start(bf16[256,512]{1,0:T(8,128)(2,1)} %get-tuple-element.140) | copy-start | bytes 786436
  136.5 16.3 %collective-permute-start.22 = (bf16[256,1024]{1,0:T(8,128)(2,1)}, bf16[256,1024]{1,0:T(8,128)(2,1)S(1)}, u32[]{:S(2)}, u32[]{:S(2)}) collective-permute-start(bf16[256,1024]{1,0:T(8,128)(2,1)} %get-tuple-element.130), channel_id=1, source_target_pairs={{4,12},{9,1},{6,14},{11,3},{20,28},{25,17},{22,30},{27,19}} | collective-permute-start | bytes 1572872 | tf_op jit(solution)/shard_map/ppermute | solution.py:774
  137.2 15.7 %collective-permute-start.23 = (bf16[256,1024]{1,0:T(8,128)(2,1)}, bf16[256,1024]{1,0:T(8,128)(2,1)S(1)}, u32[]{:S(2)}, u32[]{:S(2)}) collective-permute-start(bf16[256,1024]{1,0:T(8,128)(2,1)} %get-tuple-element.131), channel_id=1, source_target_pairs={{4,8},{9,5},{6,10},{11,7},{20,24},{25,21},{22,26},{27,23}} | collective-permute-start | bytes 1572872 | tf_op jit(solution)/shard_map/ppermute | solution.py:774
  152.9 18.3 %collective-permute-start.24 = (bf16[256,1024]{1,0:T(8,128)(2,1)}, bf16[256,1024]{1,0:T(8,128)(2,1)S(1)}, u32[]{:S(2)}, u32[]{:S(2)}) collective-permute-start(bf16[256,1024]{1,0:T(8,128)(2,1)} %get-tuple-element.146), channel_id=1, source_target_pairs={{4,0},{9,13},{6,2},{11,15},{20,16},{25,29},{22,18},{27,31}} | collective-permute-start | bytes 1572872 | tf_op jit(solution)/shard_map/ppermute | solution.py:774

commit v4 on v3

--- a/solution.py
+++ b/solution.py
@@ -855,10 +855,8 @@
     other2 = lax.ppermute(own0, both, over)
     own2 = product(piece2, swap_cores(piece2))
     other0 = lax.ppermute(own2, both, over)
-    squares_in, *_ = tie((squares, own0, own2))
-    sums = exchange(squares_in, root_pairs, root_steps)
-    piece3, piece1, other0, other2, *sums = tie((piece3, piece1, other0, other2, *sums))
-
+    *sums, (own0, own2) = exchange(squares, root_pairs, root_steps, lambda: (own0, own2))
+    piece3, piece1, own0 = tie((piece3, piece1, own0))
     own3 = product(piece3, swap_cores(piece3))
     other1 = lax.ppermute(own3, both, over)
     own1 = product(piece1, swap_cores(piece1))
@@ -885,11 +883,13 @@
     out3, out2, dq1, dq2, dq3, *terms = tie((out3, out2, dq1, dq2, dq3, *terms))
 
     out3, out2 = home(out3, 3), home(out2, 2)
-    out1, out0 = call_pull_key((1, 0), entries, slots, kept, key_gain, wa, wb, terms)
+    (out1,) = call_pull_key((1,), entries, slots, kept, key_gain, wa, wb, terms)
     d_queries = jnp.where(is_root, dq0, dq1 + dq2 + dq3)
-    out3, out2, out1, out0, d_queries = tie((out3, out2, out1, out0, d_queries))
-
-    pair = jnp.where(is_root, out0, home(out1, 1) + out2 + out3)
+    out3, out2, out1, d_queries, *terms = tie((out3, out2, out1, d_queries, *terms))
+
+    out1 = home(out1, 1)
+    (out0,) = call_pull_key((0,), entries, slots, kept, key_gain, wa, wb, terms)
+    pair = jnp.where(is_root, out0, out1 + out2 + out3)
     return d_queries, pair[:, :width], pair[:, width:]
 
 

time: 173 us -> 170 us (0.983)
  waiting for transfers between devices: 45.9 us -> 34.5 us
  Pallas kernels: 73.4 us -> 78.9 us
    ppermute x6, waiting for transfers between devices: 28.7 us -> 18.7 us  [home(): return lax.ppermute(value, both, [(b, a) for a, b in to_root(j)])]
    pallas_call x6 -> x7, Pallas kernels: 73.4 us -> 78.9 us  [call(): pl.pallas_call(kernel, out_shape=out_shape, in_specs=[spec for _, spec in...]
  transfers between devices with their start and end apart: 25 -> 25, of which waited for: 4 -> 3; matrix products, arithmetic and copies ran while one was open for 6% -> 6% of each run, Pallas kernels for 36% -> 40%
where the time goes in v4:
time: 170 us; the launch traced here: 168 us
  Pallas kernels  78.9 us (46%)
  starting transfers between devices  35.9 us (21%)
  waiting for transfers between devices  34.5 us (20%)
  local copies, waits for them, and re-layouts  9.69 us (6%)
  matrix products  3.8 us (2%)
  other arithmetic  3.31 us (2%)
  between operations  1.96 us (1%)
    pallas_call x7, Pallas kernels, call(): pl.pallas_call(kernel, out_shape=out_shape, in_specs=[spec for _, spec in...  78.9 us
    ppermute x6, waiting for transfers between devices, home(): return lax.ppermute(value, both, [(b, a) for a, b in to_root(j)])  18.7 us
    ppermute x1, waiting for transfers between devices, four_line(): lax.ppermute(lax.dynamic_slice_in_dim(out_proj, group * half, half, axis=...  15.7 us
    ppermute x3, starting transfers between devices, four_line(): lax.ppermute(rows_in, both, to_root(j))  8.42 us
    ppermute x3, starting transfers between devices, piece(): lax.ppermute(columns(array, core, place == line[j]), 'tok', [(line[j], lo...  7.44 us
    ppermute x1, starting transfers between devices, four_line(): lax.ppermute(lax.dynamic_slice_in_dim(out_proj, group * half, half, axis=...  6.25 us
    ppermute x6, starting transfers between devices, home(): return lax.ppermute(value, both, [(b, a) for a, b in to_root(j)])  5.8 us
    unnamed x40, local copies, waits for them, and re-layouts  4.71 us
  transfers between devices with their start and end apart: 25, of which 3 were waited for; matrix products, arithmetic and copies ran while one was open for 6% of the time, Pallas kernels for 40%

profile of v4, /device:TPU:0, one launch (start us, length us, event | category | flops | bytes accessed | tf_op | source)
XLA Modules:
  0.0 168.1 jit_solution(4254701995830470309)
XLA Ops:
  0.6 0.0 copy-start.1
  0.6 1.1 constant_dynamic-update-slice_fusion.2
  1.8 1.0 constant_dynamic-update-slice_fusion.1
  2.7 1.0 constant_dynamic-update-slice_fusion.refs_0_
  3.7 1.6 collective-permute-start.4
  5.3 1.6 collective-permute-start.3
  6.9 5.3 %collective-permute-start.2 = (bf16[256,1536]{1,0:T(8,128)(2,1)S(1)}, bf16[256,1536]{1,0:T(8,128)(2,1)}, u32[]{:S(2)}, u32[]{:S(2)}) collective-permute-start(bf16[256,1536]{1,0:T(8,128)(2,1)S(1)} %constant_dynamic-update-slice_fusion.refs_0_), channel_id=1, source_target_pairs={{0,4},{13,9},{2,6},{15,11},{16,20},{29,25},{18,22},{31,27}} | collective-permute-start | bytes 2359304 | tf_op jit(solution)/shard_map/ppermute | solution.py:779
  12.1 1.9 %constant_dynamic-slice_fusion.4 = bf16[256,1024]{1,0:T(8,128)(2,1)} fusion(bf16[256,4096]{1,0:T(8,128)(2,1)} %param.15, s32[]{:T(128)S(6)} %select_n.74), kind=kLoop, calls=%fused_computation.16 | loop fusion | bytes 1048580 | tf_op jit(solution)/shard_map/dynamic_slice | solution.py:791
  14.0 0.7 collective-permute-start.1
  14.7 1.1 constant_dynamic-slice_fusion.5
  15.8 6.2 %collective-permute-start = (bf16[256,1024]{1,0:T(8,128)(2,1)S(1)}, bf16[256,1024]{1,0:T(8,128)(2,1)}, u32[]{:S(2)}, u32[]{:S(2)}) collective-permute-start(bf16[256,1024]{1,0:T(8,128)(2,1)S(1)} %constant_dynamic-slice_fusion.5), channel_id=1, source_target_pairs={{0,4},{12,8},{1,5},{13,9},{2,6},{14,10},{3,7},{15,11},{16,20},{28,... | collective-permute-start | bytes 1572872 | tf_op jit(solution)/shard_map/ppermute | solution.py:782
  22.0 15.7 %collective-permute-done = bf16[256,1024]{1,0:T(8,128)(2,1)} collective-permute-done((bf16[256,1024]{1,0:T(8,128)(2,1)S(1)}, bf16[256,1024]{1,0:T(8,128)(2,1)}, u32[]{:S(2)}, u32[]{:S(2)}) %collective-permute-start) | collective-permute-done | bytes 524320 | tf_op jit(solution)/shard_map/ppermute | solution.py:782
  37.7 1.6 collective-permute-start.7
  40.0 0.2 constant_dynamic-slice_fusion
  40.2 5.4 %collective-permute-start.6 = (bf16[256,1024]{1,0:T(8,128)(2,1)S(1)}, bf16[256,1024]{1,0:T(8,128)(2,1)S(1)}, u32[]{:S(2)}, u32[]{:S(2)}) collective-permute-start(bf16[256,1024]{1,0:T(8,128)(2,1)S(1)} %get-tuple-element.157), channel_id=1, source_target_pairs={{0,4},{12,8},{1,5},{13,9},{2,6},{14,10},{3,7},{15,11},{16,20},{28,... | collective-permute-start | bytes 1572872 | tf_op jit(solution)/shard_map/ppermute | solution.py:794
  45.7 1.3 collective-permute-start.5
  47.0 0.0 copy-start.2
  47.0 14.0 %gradient.1 = (f32[512,1536]{1,0:T(8,128)}, f32[8,128]{1,0:T(8,128)}, f32[1024,1024]{1,0:T(8,128)}) custom-call(bf16[256,1536]{1,0:T(8,128)(2,1)} %copy-done, bf16[256,1536]{1,0:T(8,128)(2,1)} %collective-permute-done.2.refs_1_.refs_0_, bf16[256,1536]{1,0:T(8,128)(2,1)} %collective-permute-done.3.refs_2_.refs_1_, ...), custom_call_target="tpu_custom_call" | custom-call | flops 5368709 | bytes 1048576 | tf_op jit(solution)/shard_map/gradient/pallas_call | solution.py:475
  61.1 0.7 collective-permute-start.9
  61.7 0.1 collective-permute-start.8
  61.8 2.4 %broadcast_select_fusion.1 = (bf16[512,1024]{1,0:T(8,128)(2,1)S(1)}, bf16[512,1024]{1,0:T(8,128)(2,1)S(1)}) fusion(bf16[512,1024]{1,0:T(8,128)(2,1)S(1)} %copy-done.2, pred[]{:T(512)S(6)} %eq.23, bf16[256,1024]{1,0:T(8,128)(2,1)} %collective-permute-done, bf16[256,1024]{1,0:T(8,128)(2,1)} %collective-permute-done.7, pred[]{:T(512)S(6)} %eq.24), kind=kLoop, calls=%fused_computation.6 | loop fusion | flops 5767168 | bytes 4194306 | tf_op jit(solution)/shard_map/jit(_where)/select_n | solution.py:848
  64.3 0.5 fusion.1
  64.8 0.5 convolution_add_fusion.3.refs_2_
  65.3 0.5 fusion.2
  65.8 0.5 convolution_add_fusion.2.refs_3_
  66.3 0.6 collective-permute-start.10
  66.8 0.7 collective-permute-start.16
  67.5 0.7 collective-permute-start.15
  68.2 0.1 collective-permute-start.11
  68.3 0.0 collective-permute-done.10
  68.4 0.5 fusion.3
  68.9 0.5 convolution_add_fusion.1.refs_3_
  69.3 0.0 copy-start.12
  69.4 0.8 collective-permute-start.13
  70.2 0.0 collective-permute-done.11
  70.2 0.5 fusion.4
  70.7 0.5 convolution_add_fusion.refs_2_
  71.2 0.7 collective-permute-start.14
  71.9 0.8 collective-permute-start.12
  72.8 0.5 copy-done.10
  73.4 0.2 copy-done.14
  73.6 0.8 copy-done.15
  74.4 14.7 %query_pull.2 = (f32[512,1536]{1,0:T(8,128)}, bf16[512,1536]{1,0:T(8,128)(2,1)}, bf16[512,1536]{1,0:T(8,128)(2,1)}, bf16[256,512]{1,0:T(8,128)(2,1)}, bf16[256,512]{1,0:T(8,128)(2,1)}) custom-call(bf16[256,1536]{1,0:T(8,128)(2,1)} %copy-done, bf16[256,1536]{1,0:T(8,128)(2,1)} %collective-permute-done.3.refs_2_.refs_1_, f32[256,512]{1,0:T(8,128)} %copy-done.3, ...), custom_call_target="tpu_custom_call" | custom-call | flops 5368709120 | bytes 1048576 | tf_op jit(solution)/shard_map/query_pull/pallas_call | solution.py:475
  89.1 0.8 copy-done.16
  89.9 0.2 copy-done.17
  90.1 11.4 %query_pull.3 = (f32[512,1536]{1,0:T(8,128)}, f32[8,128]{1,0:T(8,128)}, bf16[512,1024]{1,0:T(8,128)(2,1)}, bf16[512,1024]{1,0:T(8,128)(2,1)}) custom-call(bf16[256,1536]{1,0:T(8,128)(2,1)} %collective-permute-done.2.refs_1_.refs_0_, bf16[256,1536]{1,0:T(8,128)(2,1)} %collective-permute-done.4.refs_3_.refs_1_.refs_0_, f32[256,512]{1,0:T(8,128)} %copy-done.6, ...), custom_call_target="tpu_custom_call" | custom-call | flops 5368709120 | bytes 1048576 | tf_op jit(solution)/shard_map/query_pull/pallas_call | solution.py:475
  101.5 0.7 collective-permute-start.17
  102.1 0.0 copy-start.18
  102.1 5.1 %query_grad.1 = (bf16[256,512]{1,0:T(8,128)(2,1)}, bf16[256,512]{1,0:T(8,128)(2,1)}) custom-call(bf16[512,1024]{1,0:T(8,128)(2,1)} %get-tuple-element.115.mh, bf16[512,1024]{1,0:T(8,128)(2,1)} %get-tuple-element.116.ml, bf16[512,1536]{1,0:T(8,128)(2,1)} %get-tuple-element.112.refs_8_.uh, bf16[512,1536]{1,0:T(8,128)(2,1)} %get-tuple-element.113.refs_9_.ul), custom_call_target="tpu_custom_call" | custom-call | flops 1610612736 | bytes 1048576 | tf_op jit(solution)/shard_map/query_grad/pallas_call | solution.py:475
  107.2 0.7 collective-permute-start.18
  107.9 0.7 collective-permute-start.20
  108.6 1.3 collective-permute-start.19
  109.9 0.9 collective-permute-start.21
  110.9 14.2 %key_pull.3 = (bf16[256,1024]{1,0:T(8,128)(2,1)}, bf16[256,1024]{1,0:T(8,128)(2,1)}) custom-call(bf16[256,1536]{1,0:T(8,128)(2,1)} %collective-permute-done.4.refs_3_.refs_1_.refs_0_, bf16[256,1536]{1,0:T(8,128)(2,1)} %collective-permute-done.3.refs_2_.refs_1_, f32[1024,1024]{1,0:T(8,128)} %get-tuple-element.82.refs_2_.refs_1_, ...), custom_call_target="tpu_custom_call" | custom-call | flops 6979321856 | bytes 1048576 | tf_op jit(solution)/shard_map/key_pull/pallas_call | solution.py:475
  125.1 11.0 %collective-permute-done.19 = bf16[256,512]{1,0:T(8,128)(2,1)S(1)} collective-permute-done((bf16[256,512]{1,0:T(8,128)(2,1)}, bf16[256,512]{1,0:T(8,128)(2,1)S(1)}, u32[]{:S(2)}, u32[]{:S(2)}) %collective-permute-start.19) | collective-permute-done | bytes 262176 | tf_op jit(solution)/shard_map/ppermute | solution.py:774
  136.1 0.7 collective-permute-start.22
  136.8 0.7 collective-permute-start.23
  137.5 0.8 add_select_fusion.1
  138.3 9.8 %key_pull.4 = bf16[256,1024]{1,0:T(8,128)(2,1)} custom-call(bf16[256,1536]{1,0:T(8,128)(2,1)} %collective-permute-done.2.refs_1_.refs_0_, f32[1024,1024]{1,0:T(8,128)} %get-tuple-element.82.refs_2_.refs_1_, f32[1]{0:T(128)S(6)} %copy.13.refs_4_.refs_3_.refs_2_, bf16[512,1024]{1,0:T(8,128)(2,1)} %bitcast.21, bf16[512,512]{1,0:T(8,128)(2,1)} %bitcast.26, ...), custom_call_target="tpu_custom_call" | custom-call | flops 3489660928 | bytes 1048576 | tf_op jit(solution)/shard_map/key_pull/pallas_call | solution.py:475
  148.1 1.6 collective-permute-start.24
  149.6 9.8 %key_pull.5 = bf16[256,1024]{1,0:T(8,128)(2,1)} custom-call(bf16[256,1536]{1,0:T(8,128)(2,1)} %copy-done, f32[1024,1024]{1,0:T(8,128)} %get-tuple-element.82.refs_2_.refs_1_, f32[1]{0:T(128)S(6)} %copy.13.refs_4_.refs_3_.refs_2_, bf16[512,1024]{1,0:T(8,128)(2,1)} %bitcast.22, bf16[512,512]{1,0:T(8,128)(2,1)} %bitcast.27, f32[8,128]{1,0:T(8,128)} %copy-done.8, ...), custom_call_target="tpu_custom_call" | custom-call | flops 3489660928 | bytes 1048576 | tf_op jit(solution)/shard_map/key_pull/pallas_call | solution.py:475
  159.4 7.7 %collective-permute-done.24 = bf16[256,1024]{1,0:T(8,128)(2,1)S(1)} collective-permute-done((bf16[256,1024]{1,0:T(8,128)(2,1)}, bf16[256,1024]{1,0:T(8,128)(2,1)S(1)}, u32[]{:S(2)}, u32[]{:S(2)}) %collective-permute-start.24) | collective-permute-done | bytes 524320 | tf_op jit(solution)/shard_map/ppermute | solution.py:774
  167.1 0.1 add_select_fusion
  167.2 0.8 fusion
  (51 shorter events, 0.1 us)
Async XLA Ops:
  0.6 39.4 %copy-start.1 = (bf16[256,4096]{1,0:T(8,128)(2,1)S(1)}, bf16[256,4096]{1,0:T(8,128)(2,1)}, u32[]{:S(2)}) copy-start(bf16[256,4096]{1,0:T(8,128)(2,1)} %param.15) | copy-start | bytes 6291460
  3.7 36.5 %copy-start = (bf16[256,1536]{1,0:T(8,128)(2,1)}, bf16[256,1536]{1,0:T(8,128)(2,1)S(1)}, u32[]{:S(2)}) copy-start(bf16[256,1536]{1,0:T(8,128)(2,1)S(1)} %constant_dynamic-update-slice_fusion.refs_0_) | copy-start | bytes 2359300
  3.7 34.0 %collective-permute-start.4 = (bf16[256,1536]{1,0:T(8,128)(2,1)S(1)}, bf16[256,1536]{1,0:T(8,128)(2,1)}, u32[]{:S(2)}, u32[]{:S(2)}) collective-permute-start(bf16[256,1536]{1,0:T(8,128)(2,1)S(1)} %constant_dynamic-update-slice_fusion.refs_0_), channel_id=1, source_target_pairs={{12,4},{1,9},{14,6},{3,11},{28,20},{17,25},{30,22},{19,27}} | collective-permute-start | bytes 2359304 | tf_op jit(solution)/shard_map/ppermute | solution.py:779
  5.3 32.4 %collective-permute-start.3 = (bf16[256,1536]{1,0:T(8,128)(2,1)S(1)}, bf16[256,1536]{1,0:T(8,128)(2,1)}, u32[]{:S(2)}, u32[]{:S(2)}) collective-permute-start(bf16[256,1536]{1,0:T(8,128)(2,1)S(1)} %constant_dynamic-update-slice_fusion.refs_0_), channel_id=1, source_target_pairs={{8,4},{5,9},{10,6},{7,11},{24,20},{21,25},{26,22},{23,27}} | collective-permute-start | bytes 2359304 | tf_op jit(solution)/shard_map/ppermute | solution.py:779
  6.9 30.9 %collective-permute-start.2 = (bf16[256,1536]{1,0:T(8,128)(2,1)S(1)}, bf16[256,1536]{1,0:T(8,128)(2,1)}, u32[]{:S(2)}, u32[]{:S(2)}) collective-permute-start(bf16[256,1536]{1,0:T(8,128)(2,1)S(1)} %constant_dynamic-update-slice_fusion.refs_0_), channel_id=1, source_target_pairs={{0,4},{13,9},{2,6},{15,11},{16,20},{29,25},{18,22},{31,27}} | collective-permute-start | bytes 2359304 | tf_op jit(solution)/shard_map/ppermute | solution.py:779
  14.0 8.0 %collective-permute-start.1 = (bf16[256,1024]{1,0:T(8,128)(2,1)}, bf16[256,1024]{1,0:T(8,128)(2,1)S(1)}, u32[]{:S(2)}, u32[]{:S(2)}) collective-permute-start(bf16[256,1024]{1,0:T(8,128)(2,1)} %constant_dynamic-slice_fusion.4), channel_id=1, source_target_pairs={{8,4},{4,8},{9,5},{5,9},{10,6},{6,10},{11,7},{7,11},{24,20},{20,24... | collective-permute-start | bytes 1572872 | tf_op jit(solution)/shard_map/ppermute | solution.py:794
  15.8 21.9 %collective-permute-start = (bf16[256,1024]{1,0:T(8,128)(2,1)S(1)}, bf16[256,1024]{1,0:T(8,128)(2,1)}, u32[]{:S(2)}, u32[]{:S(2)}) collective-permute-start(bf16[256,1024]{1,0:T(8,128)(2,1)S(1)} %constant_dynamic-slice_fusion.5), channel_id=1, source_target_pairs={{0,4},{12,8},{1,5},{13,9},{2,6},{14,10},{3,7},{15,11},{16,20},{28,... | collective-permute-start | bytes 1572872 | tf_op jit(solution)/shard_map/ppermute | solution.py:782
  37.7 23.3 %collective-permute-start.7 = (bf16[256,1024]{1,0:T(8,128)(2,1)}, bf16[256,1024]{1,0:T(8,128)(2,1)}, u32[]{:S(2)}, u32[]{:S(2)}) collective-permute-start(bf16[256,1024]{1,0:T(8,128)(2,1)} %collective-permute-done), channel_id=1, source_target_pairs={{0,16},{16,0},{1,17},{17,1},{2,18},{18,2},{3,19},{19,3},{4,20},{20... | collective-permute-start | bytes 1572872 | tf_op jit(solution)/shard_map/ppermute | solution.py:803
  40.2 26.0 %collective-permute-start.6 = (bf16[256,1024]{1,0:T(8,128)(2,1)S(1)}, bf16[256,1024]{1,0:T(8,128)(2,1)S(1)}, u32[]{:S(2)}, u32[]{:S(2)}) collective-permute-start(bf16[256,1024]{1,0:T(8,128)(2,1)S(1)} %get-tuple-element.157), channel_id=1, source_target_pairs={{0,4},{12,8},{1,5},{13,9},{2,6},{14,10},{3,7},{15,11},{16,20},{28,... | collective-permute-start | bytes 1572872 | tf_op jit(solution)/shard_map/ppermute | solution.py:794
  45.7 20.6 %collective-permute-start.5 = (bf16[256,1024]{1,0:T(8,128)(2,1)S(1)}, bf16[256,1024]{1,0:T(8,128)(2,1)S(1)}, u32[]{:S(2)}, u32[]{:S(2)}) collective-permute-start(bf16[256,1024]{1,0:T(8,128)(2,1)S(1)} %get-tuple-element.158), channel_id=1, source_target_pairs={{12,4},{0,8},{13,5},{1,9},{14,6},{2,10},{15,7},{3,11},{28,20},{16,... | collective-permute-start | bytes 1572872 | tf_op jit(solution)/shard_map/ppermute | solution.py:794
  47.0 14.8 %copy-start.2 = (bf16[512,1024]{1,0:T(8,128)(2,1)S(1)}, bf16[512,1024]{1,0:T(8,128)(2,1)}, u32[]{:S(2)}) copy-start(bf16[512,1024]{1,0:T(8,128)(2,1)} %param.14) | copy-start | bytes 3145732
  61.1 5.2 %collective-permute-start.9 = (f32[8,128]{1,0:T(8,128)}, f32[8,128]{1,0:T(8,128)S(1)}, u32[]{:S(2)}, u32[]{:S(2)}) collective-permute-start(f32[8,128]{1,0:T(8,128)} %get-tuple-element.93), channel_id=1, source_target_pairs={{4,9},{9,4},{6,11},{11,6},{20,25},{25,20},{22,27},{27,22}} | collective-permute-start | bytes 12296 | tf_op jit(solution)/shard_map/ppermute | solution.py:806
  61.7 3.5 %collective-permute-start.8 = (bf16[256,1024]{1,0:T(8,128)(2,1)S(1)}, bf16[256,1024]{1,0:T(8,128)(2,1)S(1)}, u32[]{:S(2)}, u32[]{:S(2)}) collective-permute-start(bf16[256,1024]{1,0:T(8,128)(2,1)S(1)} %collective-permute-done.1), channel_id=1, source_target_pairs={{0,1},{1,0},{2,3},{3,2},{4,5},{5,4},{6,7},{7,6},{8,9},{9,8},{10,11... | collective-permute-start | bytes 1572872 | tf_op jit(solution)/shard_map/ppermute | solution.py:799
  65.3 1.6 copy-start.3
  66.2 3.1 %copy-start.4 = (f32[256,512]{1,0:T(8,128)}, f32[256,512]{1,0:T(8,128)S(1)}, u32[]{:S(2)}) copy-start(f32[256,512]{1,0:T(8,128)S(1)} %convolution_add_fusion.2.refs_3_) | copy-start | bytes 1572868
  66.3 2.1 %collective-permute-start.10 = (bf16[256,1024]{1,0:T(8,128)(2,1)S(1)}, bf16[256,1024]{1,0:T(8,128)(2,1)S(1)}, u32[]{:S(2)}, u32[]{:S(2)}) collective-permute-start(bf16[256,1024]{1,0:T(8,128)(2,1)S(1)} %collective-permute-done.5), channel_id=1, source_target_pairs={{0,1},{1,0},{2,3},{3,2},{4,5},{5,4},{6,7},{7,6},{8,9},{9,8},{10,11... | collective-permute-start | bytes 1572872 | tf_op jit(solution)/shard_map/ppermute | solution.py:799
  66.8 6.0 %collective-permute-start.16 = (f32[256,512]{1,0:T(8,128)S(1)}, f32[256,512]{1,0:T(8,128)S(1)}, u32[]{:S(2)}, u32[]{:S(2)}) collective-permute-start(f32[256,512]{1,0:T(8,128)S(1)} %convolution_add_fusion.3.refs_2_), channel_id=1, source_target_pairs={{8,4},{5,9},{10,6},{7,11},{24,20},{21,25},{26,22},{23,27}} | collective-permute-start | bytes 1572872 | tf_op jit(solution)/shard_map/ppermute | solution.py:855
  67.5 5.3 %collective-permute-start.15 = (f32[256,512]{1,0:T(8,128)S(1)}, f32[256,512]{1,0:T(8,128)S(1)}, u32[]{:S(2)}, u32[]{:S(2)}) collective-permute-start(f32[256,512]{1,0:T(8,128)S(1)} %convolution_add_fusion.2.refs_3_), channel_id=1, source_target_pairs={{8,4},{5,9},{10,6},{7,11},{24,20},{21,25},{26,22},{23,27}} | collective-permute-start | bytes 1572872 | tf_op jit(solution)/shard_map/ppermute | solution.py:857
  68.2 2.0 %collective-permute-start.11 = (bf16[256,1024]{1,0:T(8,128)(2,1)S(1)}, bf16[256,1024]{1,0:T(8,128)(2,1)S(1)}, u32[]{:S(2)}, u32[]{:S(2)}) collective-permute-start(bf16[256,1024]{1,0:T(8,128)(2,1)S(1)} %collective-permute-done.6), channel_id=1, source_target_pairs={{0,1},{1,0},{2,3},{3,2},{4,5},{5,4},{6,7},{7,6},{8,9},{9,8},{10,11... | collective-permute-start | bytes 1572872 | tf_op jit(solution)/shard_map/ppermute | solution.py:799
  69.3 1.8 %copy-start.5 = (f32[256,512]{1,0:T(8,128)}, f32[256,512]{1,0:T(8,128)S(1)}, u32[]{:S(2)}) copy-start(f32[256,512]{1,0:T(8,128)S(1)} %convolution_add_fusion.1.refs_3_) | copy-start | bytes 1572868
  69.3 2.5 %copy-start.12 = (f32[8,128]{1,0:T(8,128)S(1)}, f32[8,128]{1,0:T(8,128)}, u32[]{:S(2)}) copy-start(f32[8,128]{1,0:T(8,128)} %get-tuple-element.93) | copy-start | bytes 12292
  69.4 19.7 %collective-permute-start.13 = (f32[256,512]{1,0:T(8,128)S(1)}, f32[256,512]{1,0:T(8,128)S(1)}, u32[]{:S(2)}, u32[]{:S(2)}) collective-permute-start(f32[256,512]{1,0:T(8,128)S(1)} %convolution_add_fusion.1.refs_3_), channel_id=1, source_target_pairs={{8,4},{5,9},{10,6},{7,11},{24,20},{21,25},{26,22},{23,27}} | collective-permute-start | bytes 1572872 | tf_op jit(solution)/shard_map/ppermute | solution.py:861
  71.2 17.9 %copy-start.6 = (f32[256,512]{1,0:T(8,128)}, f32[256,512]{1,0:T(8,128)S(1)}, u32[]{:S(2)}) copy-start(f32[256,512]{1,0:T(8,128)S(1)} %convolution_add_fusion.refs_2_) | copy-start | bytes 1572868
  71.2 17.9 %collective-permute-start.14 = (f32[256,512]{1,0:T(8,128)S(1)}, f32[256,512]{1,0:T(8,128)S(1)}, u32[]{:S(2)}, u32[]{:S(2)}) collective-permute-start(f32[256,512]{1,0:T(8,128)S(1)} %convolution_add_fusion.refs_2_), channel_id=1, source_target_pairs={{8,4},{5,9},{10,6},{7,11},{24,20},{21,25},{26,22},{23,27}} | collective-permute-start | bytes 1572872 | tf_op jit(solution)/shard_map/ppermute | solution.py:863
  71.9 0.9 copy-start.8
  71.9 0.9 collective-permute-start.12
  72.8 0.6 copy-start.10
  72.8 0.8 copy-start.14
  73.6 0.8 copy-start.15
  89.1 0.8 copy-start.16
  89.1 1.0 copy-start.17
  101.5 5.8 %collective-permute-start.17 = (f32[8,128]{1,0:T(8,128)}, f32[8,128]{1,0:T(8,128)S(1)}, u32[]{:S(2)}, u32[]{:S(2)}) collective-permute-start(f32[8,128]{1,0:T(8,128)} %get-tuple-element.119), channel_id=1, source_target_pairs={{4,9},{9,4},{6,11},{11,6},{20,25},{25,20},{22,27},{27,22}} | collective-permute-start | bytes 12296 | tf_op jit(solution)/shard_map/ppermute | solution.py:806
  102.1 5.1 %copy-start.13 = (f32[8,128]{1,0:T(8,128)S(1)}, f32[8,128]{1,0:T(8,128)}, u32[]{:S(2)}) copy-start(f32[8,128]{1,0:T(8,128)} %get-tuple-element.119) | copy-start | bytes 12292
  102.1 5.8 %copy-start.18 = (bf16[256,512]{1,0:T(8,128)(2,1)S(1)}, bf16[256,512]{1,0:T(8,128)(2,1)}, u32[]{:S(2)}) copy-start(bf16[256,512]{1,0:T(8,128)(2,1)} %get-tuple-element.129) | copy-start | bytes 786436
  107.2 3.6 %copy-start.9 = (f32[8,128]{1,0:T(8,128)}, f32[8,128]{1,0:T(8,128)S(1)}, u32[]{:S(2)}) copy-start(f32[8,128]{1,0:T(8,128)S(1)} %add.71.refs_8_.refs_7_) | copy-start | bytes 12292
  107.2 1.4 collective-permute-start.18
  107.9 17.1 %collective-permute-start.20 = (bf16[256,512]{1,0:T(8,128)(2,1)S(1)}, bf16[256,512]{1,0:T(8,128)(2,1)S(1)}, u32[]{:S(2)}, u32[]{:S(2)}) collective-permute-start(bf16[256,512]{1,0:T(8,128)(2,1)S(1)} %copy-done.18), channel_id=1, source_target_pairs={{4,8},{9,5},{6,10},{11,7},{20,24},{25,21},{22,26},{27,23}} | collective-permute-start | bytes 786440 | tf_op jit(solution)/shard_map/ppermute | solution.py:774
  108.6 2.2 %copy-start.11 = (f32[8,128]{1,0:T(8,128)}, f32[8,128]{1,0:T(8,128)S(1)}, u32[]{:S(2)}) copy-start(f32[8,128]{1,0:T(8,128)S(1)} %collective-permute-done.18.refs_9_.refs_8_) | copy-start | bytes 12292
  108.6 27.5 %collective-permute-start.19 = (bf16[256,512]{1,0:T(8,128)(2,1)}, bf16[256,512]{1,0:T(8,128)(2,1)S(1)}, u32[]{:S(2)}, u32[]{:S(2)}) collective-permute-start(bf16[256,512]{1,0:T(8,128)(2,1)} %get-tuple-element.128), channel_id=1, source_target_pairs={{4,0},{9,13},{6,2},{11,15},{20,16},{25,29},{22,18},{27,31}} | collective-permute-start | bytes 786440 | tf_op jit(solution)/shard_map/ppermute | solution.py:774
  109.9 26.2 %collective-permute-start.21 = (bf16[256,512]{1,0:T(8,128)(2,1)}, bf16[256,512]{1,0:T(8,128)(2,1)S(1)}, u32[]{:S(2)}, u32[]{:S(2)}) collective-permute-start(bf16[256,512]{1,0:T(8,128)(2,1)} %get-tuple-element.130), channel_id=1, source_target_pairs={{4,12},{9,1},{6,14},{11,3},{20,28},{25,17},{22,30},{27,19}} | collective-permute-start | bytes 786440 | tf_op jit(solution)/shard_map/ppermute | solution.py:774
  110.9 26.6 %copy-start.7 = (bf16[256,512]{1,0:T(8,128)(2,1)S(1)}, bf16[256,512]{1,0:T(8,128)(2,1)}, u32[]{:S(2)}) copy-start(bf16[256,512]{1,0:T(8,128)(2,1)} %get-tuple-element.139) | copy-start | bytes 786436
  136.1 11.9 %collective-permute-start.22 = (bf16[256,1024]{1,0:T(8,128)(2,1)}, bf16[256,1024]{1,0:T(8,128)(2,1)S(1)}, u32[]{:S(2)}, u32[]{:S(2)}) collective-permute-start(bf16[256,1024]{1,0:T(8,128)(2,1)} %get-tuple-element.131), channel_id=1, source_target_pairs={{4,12},{9,1},{6,14},{11,3},{20,28},{25,17},{22,30},{27,19}} | collective-permute-start | bytes 1572872 | tf_op jit(solution)/shard_map/ppermute | solution.py:774
  136.8 11.3 %collective-permute-start.23 = (bf16[256,1024]{1,0:T(8,128)(2,1)}, bf16[256,1024]{1,0:T(8,128)(2,1)S(1)}, u32[]{:S(2)}, u32[]{:S(2)}) collective-permute-start(bf16[256,1024]{1,0:T(8,128)(2,1)} %get-tuple-element.132), channel_id=1, source_target_pairs={{4,8},{9,5},{6,10},{11,7},{20,24},{25,21},{22,26},{27,23}} | collective-permute-start | bytes 1572872 | tf_op jit(solution)/shard_map/ppermute | solution.py:774
  148.1 19.0 %collective-permute-start.24 = (bf16[256,1024]{1,0:T(8,128)(2,1)}, bf16[256,1024]{1,0:T(8,128)(2,1)S(1)}, u32[]{:S(2)}, u32[]{:S(2)}) collective-permute-start(bf16[256,1024]{1,0:T(8,128)(2,1)} %key_pull.4), channel_id=1, source_target_pairs={{4,0},{9,13},{6,2},{11,15},{20,16},{25,29},{22,18},{27,31}} | collective-permute-start | bytes 1572872 | tf_op jit(solution)/shard_map/ppermute | solution.py:774
